TPU v7x, 256 devices: a whole 4x4x8 slice. The times are simulated.
256 devices in a mesh: vid: 32 (over y, z_lo, core), aud: 2 (over z_hi), head: 4 (over x).
Axes of the slice: x: 4, y: 4, z: 8 (z_hi: 2, z_lo: 4; z = z_hi * 4 + z_lo), core: 2. Of those that a mesh axis runs over, the one named last changes fastest.
Arguments:
- video_query: bfloat16 [16384, 3072], P('vid', 'head'), may hold values from -9 to 9
- video_key_array: bfloat16 [16384, 3072], P('vid', 'head'), may hold values from -16 to 16
- video_value: bfloat16 [16384, 3072], P('vid', 'head'), may hold values from -6 to 6
- video_cotangent: bfloat16 [16384, 3072], P('vid', 'head'), may hold values from -6 to 6
- audio_query: bfloat16 [1024, 3072], P('aud', 'head'), may hold values from -9 to 9
- audio_key: bfloat16 [1024, 3072], P('aud', 'head'), may hold values from -16 to 16
- audio_value: bfloat16 [1024, 3072], P('aud', 'head'), may hold values from -6 to 6
- audio_cotangent: bfloat16 [1024, 3072], P('aud', 'head'), may hold values from -6 to 6
- alignment: int32 [128, 16], replicated, may hold values from 0 to 1, as said below
Outputs:
- grad_video_query: bfloat16 [16384, 3072], P('vid', 'head')
- grad_video_key: bfloat16 [16384, 3072], P('vid', 'head')
- grad_video_value: bfloat16 [16384, 3072], P('vid', 'head')
- grad_audio_query: bfloat16 [1024, 3072], P('aud', 'head')
- grad_audio_key: bfloat16 [1024, 3072], P('aud', 'head')
- grad_audio_value: bfloat16 [1024, 3072], P('aud', 'head')
Inputs may be any that keep to these rules, and one draw needn't show every extreme that they name: `alignment`: each video time block i allows a contiguous run of audio time blocks that contains block c = 16 * i // 128 and lies within blocks c - 3 to c + 3; some video block allows all seven of c - 3 to c + 3.
All inputs are finite; a program needn't handle non-finite values.
Results may differ from a plain program's by a relative error of at most 0.006.
Values may be sent and summed in bfloat16 or wider, within the bound.
No kernel may reach another device: no remote copies, remote signals or barrier semaphores. Data moves between devices by JAX's collectives and lax.ppermute only.
A program may use at most 128 MiB of HBM per device.

v0:
```python
import functools
import math

import jax
import jax.numpy as jnp
from jax import lax
from jax.experimental import pallas as pl
from jax.experimental.pallas import tpu as pltpu
from jax.sharding import Mesh
from jax.sharding import PartitionSpec as P

DH = 128
VBLK = 128
ABLK = 64
NH = 6
HALF = 3
ROWS = 512
CH = 256
SHARE = 64
SCALE = DH ** -0.5
C2 = SCALE * math.log2(math.e)
MASKED = -1e30
FLOOR = -1e29
WIDE = HALF * DH
F32 = jnp.float32
BF16 = jnp.bfloat16
STAT = ((3, 8, ROWS), F32)
BOTH = ((2, 8, ROWS), F32)

S_Y, S_Z, S_CORE, S_AUD, S_MASK = 0, 1, 2, 3, 4

MIB = 1024 * 1024


def cost(us):
    return pl.CostEstimate(flops=us * 1_000_000_000, bytes_accessed=100_000, transcendentals=0)


def limit(mib):
    return pltpu.CompilerParams(vmem_limit_bytes=mib * MIB)


def call(kernel, ins, outs, scratch, mib, us, name, scal, *arrays):
    vmem = pl.BlockSpec(memory_space=pltpu.VMEM)
    return pl.pallas_call(
        kernel,
        in_specs=[pl.BlockSpec(memory_space=pltpu.SMEM)] + [vmem] * ins,
        out_specs=[vmem] * len(outs),
        out_shape=[jax.ShapeDtypeStruct(shape, dtype) for shape, dtype in outs],
        scratch_shapes=scratch,
        compiler_params=limit(mib),
        cost_estimate=cost(us),
        name=name,
    )(scal, *arrays)


def dot_nt(a, b):
    return lax.dot_general(a, b, (((1,), (1,)), ((), ())), preferred_element_type=F32)


def dot_nn(a, b):
    return lax.dot_general(a, b, (((1,), (0,)), ((), ())), preferred_element_type=F32)


def bias_of(scal, half, i, j):
    return jnp.where(scal[S_MASK + i * 16 + half * 8 + j] > 0, 0.0, MASKED)


def chunk_active(scal, half, q):
    c = scal[S_Y] * 4 + scal[S_Z]
    first = half * 8 + q * (CH // ABLK)
    return jnp.logical_and(first <= c + 3, first + CH // ABLK - 1 >= c - 3)


def each_chunk(scal, half, body, idle=None):
    @pl.loop(0, ROWS // CH)
    def _(q):
        rows = pl.ds(pl.multiple_of(q * CH, CH), CH)
        active = chunk_active(scal, half, q)

        @pl.when(active)
        def _():
            body(q, rows)

        if idle is not None:

            @pl.when(jnp.logical_not(active))
            def _():
                idle(rows)


def each_head(body, together):
    @pl.loop(0, NH // together)
    def _(p):
        for u in range(together):
            body(together * p + u, u)


def pair_bias(scal, half, i, j):
    lane = lax.broadcasted_iota(jnp.int32, (1, 128), 1)
    return jnp.where(lane < ABLK, bias_of(scal, half, i, j), bias_of(scal, half, i, j + 1))


def head_cols(g, r):
    return pl.ds(pl.multiple_of(g * WIDE + r * DH, DH), DH)


def first_rows(held):
    for h in range(NH):
        held[h, 0:1, :] = jnp.full((1, ROWS), FLOOR, F32)
        held[h, 1:2, :] = jnp.zeros((1, ROWS), F32)
        held[h, 2:3, :] = jnp.zeros((1, ROWS), F32)


def store_rows(stat, held):
    for k in range(3):
        for h in range(NH):
            stat[k, h : h + 1, :] = held[h, k : k + 1, :]
        stat[k, NH:8, :] = jnp.ones((8 - NH, ROWS), F32)


def shared_rows(scal):
    return pl.ds(pl.multiple_of(scal[S_Y] * 128 + scal[S_CORE] * SHARE, SHARE), SHARE)


def audio_stats_kernel(scal, vk, vv, aq, ag, stat, share, held):
    half = scal[S_AUD]
    first_rows(held)

    def chunk(q, rows):
        bias = [[pair_bias(scal, half, i, q * 4 + jj * 2) for i in range(4)] for jj in range(2)]

        def head(h, u):
            hc = head_cols(0, h)
            s = dot_nt(vk[:, hc], aq[rows, hc])
            t = dot_nt(vv[:, hc], ag[rows, hc])
            for jj in range(CH // 128):
                cols = slice(jj * 128, (jj + 1) * 128)
                out = pl.ds(pl.multiple_of(q * CH + jj * 128, 128), 128)
                top = jnp.full((1, 128), FLOOR, F32)
                for i in range(4):
                    best = jnp.max(s[i * 128 : (i + 1) * 128, cols], axis=0, keepdims=True)
                    top = jnp.maximum(top, best * C2 + bias[jj][i])
                total = jnp.zeros((1, 128), F32)
                part = jnp.zeros((1, 128), F32)
                for i in range(4):
                    e = jnp.exp2(s[i * 128 : (i + 1) * 128, cols] * C2 - (top - bias[jj][i]))
                    total += jnp.sum(e, axis=0, keepdims=True)
                    part += jnp.sum(e * t[i * 128 : (i + 1) * 128, cols], axis=0, keepdims=True)
                held[h, 0:1, out] = top
                held[h, 1:2, out] = total
                held[h, 2:3, out] = part

        each_head(head, 3)

    each_chunk(scal, half, chunk)
    store_rows(stat, held)
    rows = shared_rows(scal)
    share[0] = aq[rows, :]
    share[1] = ag[rows, :]


def video_stats_kernel(scal, vq, vg, ak, av, audio_share, stat, share, held):
    half = scal[S_AUD]
    first_rows(held)

    def chunk(q, rows):
        bias = [[bias_of(scal, half, i, q * 4 + j) for j in range(4)] for i in range(4)]

        def head(h, u):
            hc = head_cols(0, h)
            s = dot_nt(ak[rows, hc], vq[:, hc])
            t = dot_nt(av[rows, hc], vg[:, hc])
            for i in range(4):
                cols = slice(i * 128, (i + 1) * 128)
                old = held[h, 0:1, cols]
                top = old
                for j in range(4):
                    best = jnp.max(s[j * 64 : (j + 1) * 64, cols], axis=0, keepdims=True)
                    top = jnp.maximum(top, best * C2 + bias[i][j])
                shrink = jnp.exp2(old - top)
                total = held[h, 1:2, cols] * shrink
                part = held[h, 2:3, cols] * shrink
                for j in range(4):
                    e = jnp.exp2(s[j * 64 : (j + 1) * 64, cols] * C2 - (top - bias[i][j]))
                    total += jnp.sum(e, axis=0, keepdims=True)
                    part += jnp.sum(e * t[j * 64 : (j + 1) * 64, cols], axis=0, keepdims=True)
                held[h, 0:1, cols] = top
                held[h, 1:2, cols] = total
                held[h, 2:3, cols] = part

        each_head(head, 3)

    each_chunk(scal, half, chunk)
    store_rows(stat, held)
    rows = shared_rows(scal)
    share[0] = audio_share[0]
    share[1] = ak[rows, :]
    share[2] = av[rows, :]
    share[3] = audio_share[1]


def statistics(kernel, name, shared, scal, *arrays):
    scratch = [pltpu.VMEM((NH, 8, ROWS), F32)]
    share = ((shared, SHARE, NH * DH), BF16)
    return call(kernel, len(arrays), [STAT, share], scratch, 24, 20, name, scal, *arrays)


def merge_kernel(final, scal, *refs):
    *ins, out = refs
    tops = [r[0] for r in ins]
    top = functools.reduce(jnp.maximum, tops)
    weights = [jnp.exp2(t - top) for t in tops]
    total = sum(r[1] * w for r, w in zip(ins, weights))
    part = sum(r[2] * w for r, w in zip(ins, weights))
    if final:
        out[0] = top + jnp.log(total) * math.log2(math.e)
        out[1] = part / total
    else:
        out[0] = top
        out[1] = total
        out[2] = part


def merge(scal, stats, final):
    kernel = functools.partial(merge_kernel, final)
    return call(kernel, len(stats), [BOTH if final else STAT], [], 4, 1, "merge", scal, *stats)[0]


def video_queries(scal, half, q, h, ak, av, vq, vg, vstat, prob, dscore):
    s = dot_nt(ak, vq)
    t = dot_nt(av, vg)
    lses = vstat[0, pl.ds(h, 1), :]
    deltas = vstat[1, pl.ds(h, 1), :]
    for i in range(4):
        cols = slice(i * 128, (i + 1) * 128)
        lse, delta = lses[:, cols], deltas[:, cols]
        for j in range(4):
            rows = slice(j * 64, (j + 1) * 64)
            p = jnp.exp2(s[rows, cols] * C2 - (lse - bias_of(scal, half, i, q * 4 + j)))
            prob[rows, cols] = p.astype(BF16)
            dscore[rows, cols] = (p * (t[rows, cols] - delta) * SCALE).astype(BF16)


def audio_queries(scal, half, q, h, aq, ag, vk, vv, astat, prob, dscore):
    s = dot_nt(vk, aq)
    t = dot_nt(vv, ag)
    lses = astat[0, pl.ds(h, 1), :]
    deltas = astat[1, pl.ds(h, 1), :]
    for jj in range(CH // 128):
        cols = slice(jj * 128, (jj + 1) * 128)
        first, second = slice(jj * 128, jj * 128 + 128), slice(CH + jj * 128, CH + jj * 128 + 128)
        lse = jnp.where(q == 0, lses[:, first], lses[:, second])
        delta = jnp.where(q == 0, deltas[:, first], deltas[:, second])
        for i in range(4):
            rows = slice(i * 128, (i + 1) * 128)
            p = jnp.exp2(s[rows, cols] * C2 - (lse - pair_bias(scal, half, i, q * 4 + jj * 2)))
            prob[rows, cols] = p.astype(BF16)
            dscore[rows, cols] = (p * (t[rows, cols] - delta) * SCALE).astype(BF16)


def own_head(scal, at):
    h = lax.rem(scal[S_CORE] * HALF + at, NH)
    return h, head_cols(0, h), at // HALF, head_cols(0, lax.rem(at, HALF))


def own_video_kernel(scal, vq, vg, ak, av, vstat, keep, send, dvq, prob, dscore, acc, sums):
    half = scal[S_AUD]
    acc[...] = jnp.zeros_like(acc)

    def chunk(q, rows):
        def head(at, u):
            h, hc, step, sc = own_head(scal, at)
            video_queries(
                scal, half, q, h, ak[rows, hc], av[rows, hc], vq[:, hc], vg[:, hc], vstat, prob.at[u], dscore.at[u]
            )
            ds = dscore[u]
            sums[step, 0, rows, sc] = dot_nn(ds, vq[:, hc]).astype(BF16)
            sums[step, 1, rows, sc] = dot_nn(prob[u], vg[:, hc]).astype(BF16)
            acc[at] += dot_nn(ak[rows, hc].T, ds)

        each_head(head, 3)

    def idle(rows):
        for step in range(2):
            for k in range(2):
                sums[step, k, rows, :] = jnp.zeros((CH, WIDE), BF16)

    each_chunk(scal, half, chunk, idle)
    keep[...] = sums[0]
    send[...] = sums[1]

    @pl.loop(0, NH)
    def _(at):
        dvq[:, own_head(scal, at)[1]] = acc[at].T


def own_audio_kernel(scal, vk, vv, aq, ag, astat, keep, send, dvk, dvv, prob, dscore, sums):
    half = scal[S_AUD]
    dvk[...] = jnp.zeros_like(dvk)
    dvv[...] = jnp.zeros_like(dvv)

    def chunk(q, rows):
        def head(at, u):
            h, hc, step, sc = own_head(scal, at)
            audio_queries(
                scal, half, q, h, aq[rows, hc], ag[rows, hc], vk[:, hc], vv[:, hc], astat, prob.at[u], dscore.at[u]
            )
            ds = dscore[u]
            sums[step, 0, rows, sc] = dot_nn(vk[:, hc].T, ds).T.astype(BF16)
            dvk[:, hc] += dot_nn(ds, aq[rows, hc])
            dvv[:, hc] += dot_nn(prob[u], ag[rows, hc])

        each_head(head, 3)

    def idle(rows):
        for step in range(2):
            sums[step, 0, rows, :] = jnp.zeros((CH, WIDE), BF16)

    each_chunk(scal, half, chunk, idle)
    keep[...] = sums[0]
    send[...] = sums[1]


MINE = (ROWS, NH * DH)


def own_video(scal, vq, vg, ak, av, vstat):
    part = ((2, ROWS, WIDE), BF16)
    scratch = [pltpu.VMEM((3, CH, ROWS), BF16)] * 2 + [pltpu.VMEM((NH, DH, ROWS), F32)]
    scratch += [pltpu.VMEM((2, 2, ROWS, WIDE), BF16)]
    return call(
        own_video_kernel, 5, [part, part, (MINE, F32)], scratch, 28, 20, "own_video",
        scal, vq, vg, ak, av, vstat,
    )


def own_audio(scal, vk, vv, aq, ag, astat):
    part = ((1, ROWS, WIDE), BF16)
    scratch = [pltpu.VMEM((3, ROWS, CH), BF16)] * 2 + [pltpu.VMEM((2, 1, ROWS, WIDE), BF16)]
    return call(
        own_audio_kernel, 5, [part, part, (MINE, F32), (MINE, F32)], scratch, 28, 20, "own_audio",
        scal, vk, vv, aq, ag, astat,
    )


def collect(scal, pieces, audio, which):
    for d in range(4):
        y = lax.rem(scal[S_Y] + 4 - d, 4)
        for swapped in range(2):
            core = scal[S_CORE] if swapped == 0 else 1 - scal[S_CORE]
            row = pl.multiple_of(y * 128 + core * SHARE, SHARE)
            for at, k in enumerate(which):
                audio[at, pl.ds(row, SHARE), :] = pieces[2 * d + swapped][k]


def other_video_kernel(scal, vq, vg, vstat, pvq, *refs):
    pieces, (dvq, audio, prob, dscore, acc) = refs[:8], refs[8:]
    half = 1 - scal[S_AUD]
    collect(scal, pieces, audio, (1, 2))
    acc[...] = jnp.zeros_like(acc)

    def chunk(q, rows):
        def head(h, u):
            hc = head_cols(0, h)
            ak, av = audio[0, rows, hc], audio[1, rows, hc]
            video_queries(scal, half, q, h, ak, av, vq[:, hc], vg[:, hc], vstat, prob.at[u], dscore.at[u])
            acc[h] += dot_nn(ak.T, dscore[u])

        each_head(head, 2)

    each_chunk(scal, half, chunk)

    @pl.loop(0, NH)
    def _(h):
        hc = head_cols(0, h)
        dvq[:, hc] = (pvq[:, hc] + acc[h].T).astype(BF16)


def other_audio_kernel(scal, vk, vv, astat, pvk, pvv, *refs):
    pieces, (dvk, dvv, audio, prob, dscore, acck, accv) = refs[:8], refs[8:]
    half = 1 - scal[S_AUD]
    collect(scal, pieces, audio, (0, 3))
    acck[...] = pvk[...]
    accv[...] = pvv[...]

    def chunk(q, rows):
        def head(h, u):
            hc = head_cols(0, h)
            aq, ag = audio[0, rows, hc], audio[1, rows, hc]
            audio_queries(scal, half, q, h, aq, ag, vk[:, hc], vv[:, hc], astat, prob.at[u], dscore.at[u])
            acck[:, hc] += dot_nn(dscore[u], aq)
            accv[:, hc] += dot_nn(prob[u], ag)

        each_head(head, 2)

    each_chunk(scal, half, chunk)
    dvk[...] = acck[...].astype(BF16)
    dvv[...] = accv[...].astype(BF16)


def other_video(scal, vq, vg, vstat, pvq, pieces):
    scratch = [pltpu.VMEM((2,) + MINE, BF16)] + [pltpu.VMEM((2, CH, ROWS), BF16)] * 2
    scratch += [pltpu.VMEM((NH, DH, ROWS), F32)]
    return call(
        other_video_kernel, 12, [(MINE, BF16)], scratch, 28, 20, "other_video",
        scal, vq, vg, vstat, pvq, *pieces,
    )[0]


def other_audio(scal, vk, vv, astat, pvk, pvv, pieces):
    scratch = [pltpu.VMEM((2,) + MINE, BF16)] + [pltpu.VMEM((2, ROWS, CH), BF16)] * 2
    scratch += [pltpu.VMEM(MINE, F32)] * 2
    return call(
        other_audio_kernel, 13, [(MINE, BF16), (MINE, BF16)], scratch, 28, 20, "other_audio",
        scal, vk, vv, astat, pvk, pvv, *pieces,
    )


def shift(x, axis, d):
    return lax.ppermute(x, axis, [(i, (i + d) % 4) for i in range(4)])


def swap(x, axis):
    return lax.ppermute(x, axis, [(0, 1), (1, 0)])


def along(x, axis, held=None):
    return [x if held is None else after(x, held)] + [shift(x, axis, d) for d in (1, 2, 3)]


def shards(cut, axis):
    return [cut[0]] + [shift(cut[d], axis, d) for d in (1, 2, 3)]


def both_cores(parts):
    return [p for part in parts for p in (part, swap(part, "core"))]


def after(x, *others):
    return lax.optimization_barrier((x, *others))[0]


def add_kernel(groups, axis, size, scal, *refs):
    outs = refs[sum(groups) :]
    at = 0
    first = 0
    for count in groups:
        ins = refs[at : at + count]
        n = ins[0].shape[0]
        for d, out in enumerate(outs):
            if size is None:
                rows = slice(None)
            else:
                rows = pl.ds(pl.multiple_of(lax.rem(scal[axis] + d, 4) * size, size), size)
            total = sum(r[:, rows, :].astype(F32) for r in ins)
            out[first : first + n] = total.astype(BF16)
        at += count
        first += n


def add_and_cut(scal, groups, axis):
    parts = [part for group in groups for part in group]
    n = sum(group[0].shape[0] for group in groups)
    _, rows, width = parts[0].shape
    size = None if axis is None else rows // 4
    outs = 1 if axis is None else 4
    shape = jax.ShapeDtypeStruct((n, rows if axis is None else size, width), BF16)
    return pl.pallas_call(
        functools.partial(add_kernel, [len(group) for group in groups], axis, size),
        in_specs=[pl.BlockSpec(memory_space=pltpu.SMEM)] + [pl.BlockSpec(memory_space=pltpu.VMEM)] * len(parts),
        out_specs=[pl.BlockSpec(memory_space=pltpu.VMEM)] * outs,
        out_shape=[shape] * outs,
        compiler_params=limit(8),
        cost_estimate=cost(1),
        name="add_and_cut",
    )(scal, *parts)


def place_kernel(n, scal, *refs):
    pieces, outs = refs[:8], refs[8:]
    for d in range(4):
        y = lax.rem(scal[S_Y] + 4 - d, 4)
        for swapped in range(2):
            core = scal[S_CORE] if swapped == 0 else 1 - scal[S_CORE]
            cols = pl.ds(pl.multiple_of(core * (HALF * DH), HALF * DH), HALF * DH)
            for e in range(4):
                z = lax.rem(scal[S_Z] + 4 - e, 4)
                row = pl.multiple_of(y * 128 + z * 32, 32)
                for k in range(n):
                    outs[k][pl.ds(row, 32), cols] = pieces[2 * d + swapped][e, k]


def place(scal, pieces):
    n = pieces[0].shape[1]
    shape = jax.ShapeDtypeStruct((ROWS, NH * DH), BF16)
    return pl.pallas_call(
        functools.partial(place_kernel, n),
        in_specs=[pl.BlockSpec(memory_space=pltpu.SMEM)] + [pl.BlockSpec(memory_space=pltpu.VMEM)] * 8,
        out_specs=[pl.BlockSpec(memory_space=pltpu.VMEM)] * n,
        out_shape=[shape] * n,
        compiler_params=limit(8),
        cost_estimate=cost(1),
        name="place",
    )(scal, *pieces)


def per_device(vq, vk, vv, vg, aq, ak, av, ag, alignment):
    y, z, core, aud = (lax.axis_index(name) for name in ("y", "z", "core", "aud"))
    vid = (y * 4 + z) * 2 + core
    mask = lax.dynamic_slice(alignment, (vid * 4, 0), (4, 16)).reshape(64)
    scal = jnp.concatenate([jnp.stack([y, z, core, aud]).astype(jnp.int32), mask])

    apart, share = statistics(audio_stats_kernel, "audio_stats", 2, scal, vk, vv, aq, ag)
    vpart, share = statistics(video_stats_kernel, "video_stats", 4, after(scal, apart), vq, vg, ak, av, share)
    apart = merge(scal, [after(apart, vpart), swap(apart, "core")], False)
    apart = merge(scal, along(apart, "z"), False)
    vstat = merge(scal, [vpart, swap(vpart, "aud")], True)
    keep_v, send_v, dvq = own_video(after(scal, apart), vq, vg, ak, av, vstat)
    astat = merge(scal, along(apart, "y", dvq), True)
    share = swap(after(share, astat), "aud")
    astat_other = swap(astat, "aud")
    keep_a, send_a, dvk, dvv = own_audio(scal, vk, vv, aq, ag, astat)
    share = after(share, dvk)
    send_a = after(send_a, astat_other)
    cut = add_and_cut(scal, [[keep_v, swap(send_v, "core")], [keep_a, swap(send_a, "core")]], S_Y)
    shards_y = shards(cut, "y")
    cut = add_and_cut(scal, [shards_y], S_Z)
    share = after(share, shards_y[1])
    own, first, third = share, shift(share, "y", 1), shift(share, "y", 3)
    shards_z = shards(cut, "z")
    piece = add_and_cut(scal, [shards_z], None)[0]
    second = shift(after(share, piece), "y", 2)
    line = jnp.stack(along(after(piece, first, third), "z"))
    pieces = both_cores([own, first, after(second, line), third])
    dvq = other_video(after(scal, line), vq, vg, vstat, dvq, pieces)
    dvk, dvv = other_audio(after(scal, dvq), vk, vv, astat_other, dvk, dvv, pieces)
    gathered = along(line, "y")
    gathered = both_cores(gathered[:1]) + both_cores([after(part, dvk) for part in gathered[1:]])
    dak, dav, daq = place(scal, gathered)
    return dvq, dvk, dvv, daq, dak, dav


def solution(mesh):
    grid = Mesh(mesh.devices.reshape(4, 4, 2, 2, 4), ("y", "z", "core", "aud", "head"))
    video = P(("y", "z", "core"), "head")
    audio = P("aud", "head")
    return jax.shard_map(
        per_device,
        mesh=grid,
        in_specs=(video,) * 4 + (audio,) * 4 + (P(),),
        out_specs=(video,) * 3 + (audio,) * 3,
        check_vma=False,
    )
```

profile of v0, /device:TPU:55, one launch (start us, length us, event | category | flops | bytes accessed | tf_op | source)
XLA Modules:
  0.0 122.3 jit_solution(12982272814483858693)
XLA Ops:
  1.7 1.1 copy-done.3
  6.2 2.2 %audio_stats.1 = (f32[3,8,512]{2,1,0:T(8,128)S(1)}, bf16[2,64,768]{2,1,0:T(8,128)(2,1)S(1)}) custom-call(s32[68]{0:T(128)S(1)} %concatenate.3.scal, bf16[512,768]{1,0:T(8,128)(2,1)S(1)} %copy-done.9, bf16[512,768]{1,0:T(8,128)(2,1)S(1)} %copy-done.11, bf16[512,768]{1,0:T(8,128)(2,1)S(1)} %copy-done.3, bf16[512,768]{1,0:T(8,128)(2,1)S(1)} %copy-done.5), custom_call_target="tpu_custom_call" | custom-call | flops 20000000000 | bytes 100000 | tf_op jit(solution)/shard_map/audio_stats/pallas_call | solution.py:45
  9.2 2.2 %video_stats.1 = (f32[3,8,512]{2,1,0:T(8,128)S(1)}, bf16[4,64,768]{2,1,0:T(8,128)(2,1)S(1)}) custom-call(s32[68]{0:T(128)S(1)} %concatenate.3.scal, bf16[512,768]{1,0:T(8,128)(2,1)S(1)} %copy-done.7, bf16[512,768]{1,0:T(8,128)(2,1)S(1)} %copy-done.8, bf16[512,768]{1,0:T(8,128)(2,1)S(1)} %copy-done.1, bf16[512,768]{1,0:T(8,128)(2,1)S(1)} %copy-done.2, ...), custom_call_target="tpu_custom_call" | custom-call | flops 20000000000 | bytes 100000 | tf_op jit(solution)/shard_map/video_stats/pallas_call | solution.py:45
  11.5 9.4 %collective-permute-start.4 = (f32[3,8,512]{2,1,0:T(8,128)S(1)}, f32[3,8,512]{2,1,0:T(8,128)S(1)}, u32[]{:S(2)}, u32[]{:S(2)}) collective-permute-start(f32[3,8,512]{2,1,0:T(8,128)S(1)} %get-tuple-element.49.refs_0_), channel_id=1, source_target_pairs={{0,4},{4,0},{1,5},{5,1},{2,6},{6,2},{3,7},{7,3},{8,12},{12,8},{9,1... | collective-permute-start | bytes 147464 | tf_op jit(solution)/shard_map/ppermute | solution.py:425
  22.8 1.4 %collective-permute-start.3 = (f32[3,8,512]{2,1,0:T(8,128)S(1)}, f32[3,8,512]{2,1,0:T(8,128)S(1)}, u32[]{:S(2)}, u32[]{:S(2)}) collective-permute-start(f32[3,8,512]{2,1,0:T(8,128)S(1)} %merge.4.refs_0_), channel_id=1, source_target_pairs={{0,48},{16,0},{32,16},{48,32},{1,49},{17,1},{33,17},{49,33},{2,50}... | collective-permute-start | bytes 147464 | tf_op jit(solution)/shard_map/ppermute | solution.py:421
  24.7 1.3 %collective-permute-done.2.refs_2_ = f32[3,8,512]{2,1,0:T(8,128)S(1)} collective-permute-done((f32[3,8,512]{2,1,0:T(8,128)S(1)}, f32[3,8,512]{2,1,0:T(8,128)S(1)}, u32[]{:S(2)}, u32[]{:S(2)}) %collective-permute-start.2) | collective-permute-done | bytes 49184 | tf_op jit(solution)/shard_map/ppermute | solution.py:421
  26.1 2.1 %collective-permute-done.3.refs_3_ = f32[3,8,512]{2,1,0:T(8,128)S(1)} collective-permute-done((f32[3,8,512]{2,1,0:T(8,128)S(1)}, f32[3,8,512]{2,1,0:T(8,128)S(1)}, u32[]{:S(2)}, u32[]{:S(2)}) %collective-permute-start.3) | collective-permute-done | bytes 49184 | tf_op jit(solution)/shard_map/ppermute | solution.py:421
  28.8 2.2 %collective-permute-start.6 = (f32[3,8,512]{2,1,0:T(8,128)S(1)}, f32[3,8,512]{2,1,0:T(8,128)S(1)}, u32[]{:S(2)}, u32[]{:S(2)}) collective-permute-start(f32[3,8,512]{2,1,0:T(8,128)S(1)} %merge.5.refs_0_), channel_id=1, source_target_pairs={{0,64},{64,128},{128,192},{192,0},{1,65},{65,129},{129,193},{193,1... | collective-permute-start | bytes 147464 | tf_op jit(solution)/shard_map/ppermute | solution.py:421
  31.0 1.3 %collective-permute-start.8 = (f32[3,8,512]{2,1,0:T(8,128)S(1)}, f32[3,8,512]{2,1,0:T(8,128)S(1)}, u32[]{:S(2)}, u32[]{:S(2)}) collective-permute-start(f32[3,8,512]{2,1,0:T(8,128)S(1)} %merge.5.refs_0_), channel_id=1, source_target_pairs={{0,192},{64,0},{128,64},{192,128},{1,193},{65,1},{129,65},{193,129... | collective-permute-start | bytes 147464 | tf_op jit(solution)/shard_map/ppermute | solution.py:421
  32.3 4.5 %own_video.1 = (bf16[2,512,384]{2,1,0:T(8,128)(2,1)S(1)}, bf16[2,512,384]{2,1,0:T(8,128)(2,1)S(1)}, f32[512,768]{1,0:T(8,128)S(1)}) custom-call(s32[68]{0:T(128)S(1)} %concatenate.3.scal, bf16[512,768]{1,0:T(8,128)(2,1)S(1)} %copy-done.7, bf16[512,768]{1,0:T(8,128)(2,1)S(1)} %copy-done.8, bf16[512,768]{1,0:T(8,128)(2,1)S(1)} %copy-done.1, ...), custom_call_target="tpu_custom_call" | custom-call | flops 20000000000 | bytes 100000 | tf_op jit(solution)/shard_map/own_video/pallas_call | solution.py:45
  36.8 1.3 %collective-permute-start.5 = (bf16[2,512,384]{2,1,0:T(8,128)(2,1)S(1)}, bf16[2,512,384]{2,1,0:T(8,128)(2,1)S(1)}, u32[]{:S(2)}, u32[]{:S(2)}) collective-permute-start(bf16[2,512,384]{2,1,0:T(8,128)(2,1)S(1)} %get-tuple-element.53), channel_id=1, source_target_pairs={{0,8},{8,0},{1,9},{9,1},{2,10},{10,2},{3,11},{11,3},{4,12},{12,4},... | collective-permute-start | bytes 2359304 | tf_op jit(solution)/shard_map/ppermute | solution.py:425
  38.7 4.0 %collective-permute-start.9 = (f32[2,8,512]{2,1,0:T(8,128)S(1)}, f32[2,8,512]{2,1,0:T(8,128)S(1)}, u32[]{:S(2)}, u32[]{:S(2)}) collective-permute-start(f32[2,8,512]{2,1,0:T(8,128)S(1)} %merge.7.astat), channel_id=1, source_target_pairs={{0,4},{4,0},{1,5},{5,1},{2,6},{6,2},{3,7},{7,3},{8,12},{12,8},{9,1... | collective-permute-start | bytes 98312 | tf_op jit(solution)/shard_map/ppermute | solution.py:425
  42.7 4.2 %own_audio.1 = (bf16[1,512,384]{2,1,0:T(8,128)(2,1)S(1)}, bf16[1,512,384]{2,1,0:T(8,128)(2,1)S(1)}, f32[512,768]{1,0:T(8,128)S(1)}, f32[512,768]{1,0:T(8,128)S(1)}) custom-call(s32[68]{0:T(128)S(1)} %concatenate.3.scal, bf16[512,768]{1,0:T(8,128)(2,1)S(1)} %copy-done.10, bf16[512,768]{1,0:T(8,128)(2,1)S(1)} %copy-done.12, bf16[512,768]{1,0:T(8,128)(2,1)S(1)} %copy-done.4, ...), custom_call_target="tpu_custom_call" | custom-call | flops 20000000000 | bytes 100000 | tf_op jit(solution)/shard_map/own_audio/pallas_call | solution.py:45
  47.5 4.8 %collective-permute-start.17 = (bf16[4,64,768]{2,1,0:T(8,128)(2,1)S(1)}, bf16[4,64,768]{2,1,0:T(8,128)(2,1)S(1)}, u32[]{:S(2)}, u32[]{:S(2)}) collective-permute-start(bf16[4,64,768]{2,1,0:T(8,128)(2,1)S(1)} %get-tuple-element.68), channel_id=1, source_target_pairs={{0,4},{4,0},{1,5},{5,1},{2,6},{6,2},{3,7},{7,3},{8,12},{12,8},{9,1... | collective-permute-start | bytes 1179656 | tf_op jit(solution)/shard_map/ppermute | solution.py:425
  53.1 1.1 collective-permute-start.11
  54.3 1.8 %collective-permute-start.12 = (bf16[3,128,384]{2,1,0:T(8,128)(2,1)S(1)}, bf16[3,128,384]{2,1,0:T(8,128)(2,1)S(1)}, u32[]{:S(2)}, u32[]{:S(2)}) collective-permute-start(bf16[3,128,384]{2,1,0:T(8,128)(2,1)S(1)} %get-tuple-element.61), channel_id=1, source_target_pairs={{0,128},{64,192},{128,0},{192,64},{1,129},{65,193},{129,1},{193,65... | collective-permute-start | bytes 884744 | tf_op jit(solution)/shard_map/ppermute | solution.py:421
  56.8 14.0 %collective-permute-done.17.refs_0_ = bf16[4,64,768]{2,1,0:T(8,128)(2,1)S(1)} collective-permute-done((bf16[4,64,768]{2,1,0:T(8,128)(2,1)S(1)}, bf16[4,64,768]{2,1,0:T(8,128)(2,1)S(1)}, u32[]{:S(2)}, u32[]{:S(2)}) %collective-permute-start.17) | collective-permute-done | bytes 393248 | tf_op jit(solution)/shard_map/ppermute | solution.py:425
  71.2 2.3 %collective-permute-start.19 = (bf16[4,64,768]{2,1,0:T(8,128)(2,1)S(1)}, bf16[4,64,768]{2,1,0:T(8,128)(2,1)S(1)}, u32[]{:S(2)}, u32[]{:S(2)}) collective-permute-start(bf16[4,64,768]{2,1,0:T(8,128)(2,1)S(1)} %collective-permute-done.17.refs_0_), channel_id=1, source_target_pairs={{0,192},{64,0},{128,64},{192,128},{1,193},{65,1},{129,65},{193,129... | collective-permute-start | bytes 1179656 | tf_op jit(solution)/shard_map/ppermute | solution.py:421
  74.1 1.7 %collective-permute-start.14 = (bf16[3,32,384]{2,1,0:T(8,128)(2,1)S(1)}, bf16[3,32,384]{2,1,0:T(8,128)(2,1)S(1)}, u32[]{:S(2)}, u32[]{:S(2)}) collective-permute-start(bf16[3,32,384]{2,1,0:T(8,128)(2,1)S(1)} %get-tuple-element.64), channel_id=1, source_target_pairs={{0,16},{16,32},{32,48},{48,0},{1,17},{17,33},{33,49},{49,1},{2,18}... | collective-permute-start | bytes 221192 | tf_op jit(solution)/shard_map/ppermute | solution.py:421
  75.8 1.3 %collective-permute-start.16 = (bf16[3,32,384]{2,1,0:T(8,128)(2,1)S(1)}, bf16[3,32,384]{2,1,0:T(8,128)(2,1)S(1)}, u32[]{:S(2)}, u32[]{:S(2)}) collective-permute-start(bf16[3,32,384]{2,1,0:T(8,128)(2,1)S(1)} %get-tuple-element.66), channel_id=1, source_target_pairs={{0,48},{16,0},{32,16},{48,32},{1,49},{17,1},{33,17},{49,33},{2,50}... | collective-permute-start | bytes 221192 | tf_op jit(solution)/shard_map/ppermute | solution.py:421
  77.7 2.3 %collective-permute-done.15.refs_2_ = bf16[3,32,384]{2,1,0:T(8,128)(2,1)S(1)} collective-permute-done((bf16[3,32,384]{2,1,0:T(8,128)(2,1)S(1)}, bf16[3,32,384]{2,1,0:T(8,128)(2,1)S(1)}, u32[]{:S(2)}, u32[]{:S(2)}) %collective-permute-start.15) | collective-permute-done | bytes 73760 | tf_op jit(solution)/shard_map/ppermute | solution.py:421
  81.2 6.2 %collective-permute-start.25 = (bf16[4,64,768]{2,1,0:T(8,128)(2,1)S(1)}, bf16[4,64,768]{2,1,0:T(8,128)(2,1)S(1)}, u32[]{:S(2)}, u32[]{:S(2)}) collective-permute-start(bf16[4,64,768]{2,1,0:T(8,128)(2,1)S(1)} %collective-permute-done.17.refs_0_), channel_id=1, source_target_pairs={{0,128},{64,192},{128,0},{192,64},{1,129},{65,193},{129,1},{193,65... | collective-permute-start | bytes 1179656 | tf_op jit(solution)/shard_map/ppermute | solution.py:421
  88.2 1.1 collective-permute-start.22
  89.3 3.2 %collective-permute-start.23 = (bf16[4,64,768]{2,1,0:T(8,128)(2,1)S(1)}, bf16[4,64,768]{2,1,0:T(8,128)(2,1)S(1)}, u32[]{:S(2)}, u32[]{:S(2)}) collective-permute-start(bf16[4,64,768]{2,1,0:T(8,128)(2,1)S(1)} %collective-permute-done.17.refs_0_), channel_id=1, source_target_pairs={{0,8},{8,0},{1,9},{9,1},{2,10},{10,2},{3,11},{11,3},{4,12},{12,4},... | collective-permute-start | bytes 1179656 | tf_op jit(solution)/shard_map/ppermute | solution.py:425
  92.5 1.6 %collective-permute-start.24 = (bf16[4,64,768]{2,1,0:T(8,128)(2,1)S(1)}, bf16[4,64,768]{2,1,0:T(8,128)(2,1)S(1)}, u32[]{:S(2)}, u32[]{:S(2)}) collective-permute-start(bf16[4,64,768]{2,1,0:T(8,128)(2,1)S(1)} %collective-permute-done.18.refs_2_), channel_id=1, source_target_pairs={{0,8},{8,0},{1,9},{9,1},{2,10},{10,2},{3,11},{11,3},{4,12},{12,4},... | collective-permute-start | bytes 1179656 | tf_op jit(solution)/shard_map/ppermute | solution.py:425
  94.1 1.4 %collective-permute-start.27 = (bf16[4,64,768]{2,1,0:T(8,128)(2,1)S(1)}, bf16[4,64,768]{2,1,0:T(8,128)(2,1)S(1)}, u32[]{:S(2)}, u32[]{:S(2)}) collective-permute-start(bf16[4,64,768]{2,1,0:T(8,128)(2,1)S(1)} %collective-permute-done.19.refs_6_), channel_id=1, source_target_pairs={{0,8},{8,0},{1,9},{9,1},{2,10},{10,2},{3,11},{11,3},{4,12},{12,4},... | collective-permute-start | bytes 1179656 | tf_op jit(solution)/shard_map/ppermute | solution.py:425
  95.6 1.8 %collective-permute-start.26 = (bf16[4,64,768]{2,1,0:T(8,128)(2,1)S(1)}, bf16[4,64,768]{2,1,0:T(8,128)(2,1)S(1)}, u32[]{:S(2)}, u32[]{:S(2)}) collective-permute-start(bf16[4,64,768]{2,1,0:T(8,128)(2,1)S(1)} %collective-permute-done.25.refs_4_), channel_id=1, source_target_pairs={{0,8},{8,0},{1,9},{9,1},{2,10},{10,2},{3,11},{11,3},{4,12},{12,4},... | collective-permute-start | bytes 1179656 | tf_op jit(solution)/shard_map/ppermute | solution.py:425
  98.3 2.0 %collective-permute-start.31 = (bf16[4,3,32,384]{3,2,1,0:T(8,128)(2,1)S(1)}, bf16[4,3,32,384]{3,2,1,0:T(8,128)(2,1)S(1)}, u32[]{:S(2)}, u32[]{:S(2)}) collective-permute-start(bf16[4,3,32,384]{3,2,1,0:T(8,128)(2,1)S(1)} %pad_maximum_fusion.refs_0_), channel_id=1, source_target_pairs={{0,128},{64,192},{128,0},{192,64},{1,129},{65,193},{129,1},{193,65... | collective-permute-start | bytes 884744 | tf_op jit(solution)/shard_map/ppermute | solution.py:421
  100.4 2.1 %collective-permute-start.29 = (bf16[4,3,32,384]{3,2,1,0:T(8,128)(2,1)S(1)}, bf16[4,3,32,384]{3,2,1,0:T(8,128)(2,1)S(1)}, u32[]{:S(2)}, u32[]{:S(2)}) collective-permute-start(bf16[4,3,32,384]{3,2,1,0:T(8,128)(2,1)S(1)} %pad_maximum_fusion.refs_0_), channel_id=1, source_target_pairs={{0,64},{64,128},{128,192},{192,0},{1,65},{65,129},{129,193},{193,1... | collective-permute-start | bytes 884744 | tf_op jit(solution)/shard_map/ppermute | solution.py:421
  103.3 7.6 %other_video.1 = bf16[512,768]{1,0:T(8,128)(2,1)} custom-call(s32[68]{0:T(128)S(1)} %concatenate.3.scal, bf16[512,768]{1,0:T(8,128)(2,1)S(1)} %copy-done.7, bf16[512,768]{1,0:T(8,128)(2,1)S(1)} %copy-done.8, f32[2,8,512]{2,1,0:T(8,128)S(1)} %merge.6.vstat, f32[512,768]{1,0:T(8,128)S(1)} %get-tuple-element.54.pvq, ...), custom_call_target="tpu_custom_call" | custom-call | flops 20000000000 | bytes 100000 | tf_op jit(solution)/shard_map/other_video/pallas_call | solution.py:45
  110.9 6.8 %other_audio.1 = (bf16[512,768]{1,0:T(8,128)(2,1)}, bf16[512,768]{1,0:T(8,128)(2,1)}) custom-call(s32[68]{0:T(128)S(1)} %concatenate.3.scal, bf16[512,768]{1,0:T(8,128)(2,1)S(1)} %copy-done.10, bf16[512,768]{1,0:T(8,128)(2,1)S(1)} %copy-done.12, f32[2,8,512]{2,1,0:T(8,128)S(1)} %collective-permute-done.9.astat, f32[512,768]{1,0:T(8,128)S(1)} %get-tuple-element.69.pvk, ...), custom_call_target="tpu_custom_call" | custom-call | flops 20000000000 | bytes 100000 | tf_op jit(solution)/shard_map/other_audio/pallas_call | solution.py:45
  120.1 2.2 %place.1 = (bf16[512,768]{1,0:T(8,128)(2,1)}, bf16[512,768]{1,0:T(8,128)(2,1)}, bf16[512,768]{1,0:T(8,128)(2,1)}) custom-call(s32[68]{0:T(128)S(1)} %concatenate.3.scal, bf16[4,3,32,384]{3,2,1,0:T(8,128)(2,1)S(1)} %pad_maximum_fusion.refs_0_, bf16[4,3,32,384]{3,2,1,0:T(8,128)(2,1)S(1)} %collective-permute-done.28.refs_1_, ...), custom_call_target="tpu_custom_call" | custom-call | flops 1000000000 | bytes 100000 | tf_op jit(solution)/shard_map/place/pallas_call | solution.py:497
  (83 shorter events, 19.0 us)
Async XLA Ops:
  8.5 12.4 %collective-permute-start = (f32[3,8,512]{2,1,0:T(8,128)S(1)}, f32[3,8,512]{2,1,0:T(8,128)S(1)}, u32[]{:S(2)}, u32[]{:S(2)}) collective-permute-start(f32[3,8,512]{2,1,0:T(8,128)S(1)} %get-tuple-element.50.refs_0_), channel_id=1, source_target_pairs={{0,8},{8,0},{1,9},{9,1},{2,10},{10,2},{3,11},{11,3},{4,12},{12,4},... | collective-permute-start | bytes 147464 | tf_op jit(solution)/shard_map/ppermute | solution.py:425
  11.5 12.7 %collective-permute-start.4 = (f32[3,8,512]{2,1,0:T(8,128)S(1)}, f32[3,8,512]{2,1,0:T(8,128)S(1)}, u32[]{:S(2)}, u32[]{:S(2)}) collective-permute-start(f32[3,8,512]{2,1,0:T(8,128)S(1)} %get-tuple-element.49.refs_0_), channel_id=1, source_target_pairs={{0,4},{4,0},{1,5},{5,1},{2,6},{6,2},{3,7},{7,3},{8,12},{12,8},{9,1... | collective-permute-start | bytes 147464 | tf_op jit(solution)/shard_map/ppermute | solution.py:425
  21.4 3.3 %collective-permute-start.1 = (f32[3,8,512]{2,1,0:T(8,128)S(1)}, f32[3,8,512]{2,1,0:T(8,128)S(1)}, u32[]{:S(2)}, u32[]{:S(2)}) collective-permute-start(f32[3,8,512]{2,1,0:T(8,128)S(1)} %merge.4.refs_0_), channel_id=1, source_target_pairs={{0,16},{16,32},{32,48},{48,0},{1,17},{17,33},{33,49},{49,1},{2,18}... | collective-permute-start | bytes 147464 | tf_op jit(solution)/shard_map/ppermute | solution.py:421
  22.2 3.8 %collective-permute-start.2 = (f32[3,8,512]{2,1,0:T(8,128)S(1)}, f32[3,8,512]{2,1,0:T(8,128)S(1)}, u32[]{:S(2)}, u32[]{:S(2)}) collective-permute-start(f32[3,8,512]{2,1,0:T(8,128)S(1)} %merge.4.refs_0_), channel_id=1, source_target_pairs={{0,32},{16,48},{32,0},{48,16},{1,33},{17,49},{33,1},{49,17},{2,34}... | collective-permute-start | bytes 147464 | tf_op jit(solution)/shard_map/ppermute | solution.py:421
  22.8 5.4 %collective-permute-start.3 = (f32[3,8,512]{2,1,0:T(8,128)S(1)}, f32[3,8,512]{2,1,0:T(8,128)S(1)}, u32[]{:S(2)}, u32[]{:S(2)}) collective-permute-start(f32[3,8,512]{2,1,0:T(8,128)S(1)} %merge.4.refs_0_), channel_id=1, source_target_pairs={{0,48},{16,0},{32,16},{48,32},{1,49},{17,1},{33,17},{49,33},{2,50}... | collective-permute-start | bytes 147464 | tf_op jit(solution)/shard_map/ppermute | solution.py:421
  28.8 9.4 %collective-permute-start.6 = (f32[3,8,512]{2,1,0:T(8,128)S(1)}, f32[3,8,512]{2,1,0:T(8,128)S(1)}, u32[]{:S(2)}, u32[]{:S(2)}) collective-permute-start(f32[3,8,512]{2,1,0:T(8,128)S(1)} %merge.5.refs_0_), channel_id=1, source_target_pairs={{0,64},{64,128},{128,192},{192,0},{1,65},{65,129},{129,193},{193,1... | collective-permute-start | bytes 147464 | tf_op jit(solution)/shard_map/ppermute | solution.py:421
  31.0 7.1 %collective-permute-start.7 = (f32[3,8,512]{2,1,0:T(8,128)S(1)}, f32[3,8,512]{2,1,0:T(8,128)S(1)}, u32[]{:S(2)}, u32[]{:S(2)}) collective-permute-start(f32[3,8,512]{2,1,0:T(8,128)S(1)} %merge.5.refs_0_), channel_id=1, source_target_pairs={{0,128},{64,192},{128,0},{192,64},{1,129},{65,193},{129,1},{193,65... | collective-permute-start | bytes 147464 | tf_op jit(solution)/shard_map/ppermute | solution.py:421
  31.0 7.1 %collective-permute-start.8 = (f32[3,8,512]{2,1,0:T(8,128)S(1)}, f32[3,8,512]{2,1,0:T(8,128)S(1)}, u32[]{:S(2)}, u32[]{:S(2)}) collective-permute-start(f32[3,8,512]{2,1,0:T(8,128)S(1)} %merge.5.refs_0_), channel_id=1, source_target_pairs={{0,192},{64,0},{128,64},{192,128},{1,193},{65,1},{129,65},{193,129... | collective-permute-start | bytes 147464 | tf_op jit(solution)/shard_map/ppermute | solution.py:421
  36.8 15.5 %collective-permute-start.5 = (bf16[2,512,384]{2,1,0:T(8,128)(2,1)S(1)}, bf16[2,512,384]{2,1,0:T(8,128)(2,1)S(1)}, u32[]{:S(2)}, u32[]{:S(2)}) collective-permute-start(bf16[2,512,384]{2,1,0:T(8,128)(2,1)S(1)} %get-tuple-element.53), channel_id=1, source_target_pairs={{0,8},{8,0},{1,9},{9,1},{2,10},{10,2},{3,11},{11,3},{4,12},{12,4},... | collective-permute-start | bytes 2359304 | tf_op jit(solution)/shard_map/ppermute | solution.py:425
  38.7 8.3 %collective-permute-start.9 = (f32[2,8,512]{2,1,0:T(8,128)S(1)}, f32[2,8,512]{2,1,0:T(8,128)S(1)}, u32[]{:S(2)}, u32[]{:S(2)}) collective-permute-start(f32[2,8,512]{2,1,0:T(8,128)S(1)} %merge.7.astat), channel_id=1, source_target_pairs={{0,4},{4,0},{1,5},{5,1},{2,6},{6,2},{3,7},{7,3},{8,12},{12,8},{9,1... | collective-permute-start | bytes 98312 | tf_op jit(solution)/shard_map/ppermute | solution.py:425
  47.0 5.3 %collective-permute-start.10 = (bf16[1,512,384]{2,1,0:T(8,128)(2,1)S(1)}, bf16[1,512,384]{2,1,0:T(8,128)(2,1)S(1)}, u32[]{:S(2)}, u32[]{:S(2)}) collective-permute-start(bf16[1,512,384]{2,1,0:T(8,128)(2,1)S(1)} %get-tuple-element.58), channel_id=1, source_target_pairs={{0,8},{8,0},{1,9},{9,1},{2,10},{10,2},{3,11},{11,3},{4,12},{12,4},... | collective-permute-start | bytes 1179656 | tf_op jit(solution)/shard_map/ppermute | solution.py:425
  47.5 23.2 %collective-permute-start.17 = (bf16[4,64,768]{2,1,0:T(8,128)(2,1)S(1)}, bf16[4,64,768]{2,1,0:T(8,128)(2,1)S(1)}, u32[]{:S(2)}, u32[]{:S(2)}) collective-permute-start(bf16[4,64,768]{2,1,0:T(8,128)(2,1)S(1)} %get-tuple-element.68), channel_id=1, source_target_pairs={{0,4},{4,0},{1,5},{5,1},{2,6},{6,2},{3,7},{7,3},{8,12},{12,8},{9,1... | collective-permute-start | bytes 1179656 | tf_op jit(solution)/shard_map/ppermute | solution.py:425
  53.1 17.6 %collective-permute-start.11 = (bf16[3,128,384]{2,1,0:T(8,128)(2,1)S(1)}, bf16[3,128,384]{2,1,0:T(8,128)(2,1)S(1)}, u32[]{:S(2)}, u32[]{:S(2)}) collective-permute-start(bf16[3,128,384]{2,1,0:T(8,128)(2,1)S(1)} %get-tuple-element.60), channel_id=1, source_target_pairs={{0,64},{64,128},{128,192},{192,0},{1,65},{65,129},{129,193},{193,1... | collective-permute-start | bytes 884744 | tf_op jit(solution)/shard_map/ppermute | solution.py:421
  54.3 19.1 %collective-permute-start.12 = (bf16[3,128,384]{2,1,0:T(8,128)(2,1)S(1)}, bf16[3,128,384]{2,1,0:T(8,128)(2,1)S(1)}, u32[]{:S(2)}, u32[]{:S(2)}) collective-permute-start(bf16[3,128,384]{2,1,0:T(8,128)(2,1)S(1)} %get-tuple-element.61), channel_id=1, source_target_pairs={{0,128},{64,192},{128,0},{192,64},{1,129},{65,193},{129,1},{193,65... | collective-permute-start | bytes 884744 | tf_op jit(solution)/shard_map/ppermute | solution.py:421
  56.1 17.3 %collective-permute-start.13 = (bf16[3,128,384]{2,1,0:T(8,128)(2,1)S(1)}, bf16[3,128,384]{2,1,0:T(8,128)(2,1)S(1)}, u32[]{:S(2)}, u32[]{:S(2)}) collective-permute-start(bf16[3,128,384]{2,1,0:T(8,128)(2,1)S(1)} %get-tuple-element.62), channel_id=1, source_target_pairs={{0,192},{64,0},{128,64},{192,128},{1,193},{65,1},{129,65},{193,129... | collective-permute-start | bytes 884744 | tf_op jit(solution)/shard_map/ppermute | solution.py:421
  70.8 16.6 %collective-permute-start.18 = (bf16[4,64,768]{2,1,0:T(8,128)(2,1)S(1)}, bf16[4,64,768]{2,1,0:T(8,128)(2,1)S(1)}, u32[]{:S(2)}, u32[]{:S(2)}) collective-permute-start(bf16[4,64,768]{2,1,0:T(8,128)(2,1)S(1)} %collective-permute-done.17.refs_0_), channel_id=1, source_target_pairs={{0,64},{64,128},{128,192},{192,0},{1,65},{65,129},{129,193},{193,1... | collective-permute-start | bytes 1179656 | tf_op jit(solution)/shard_map/ppermute | solution.py:421
  71.2 16.2 %collective-permute-start.19 = (bf16[4,64,768]{2,1,0:T(8,128)(2,1)S(1)}, bf16[4,64,768]{2,1,0:T(8,128)(2,1)S(1)}, u32[]{:S(2)}, u32[]{:S(2)}) collective-permute-start(bf16[4,64,768]{2,1,0:T(8,128)(2,1)S(1)} %collective-permute-done.17.refs_0_), channel_id=1, source_target_pairs={{0,192},{64,0},{128,64},{192,128},{1,193},{65,1},{129,65},{193,129... | collective-permute-start | bytes 1179656 | tf_op jit(solution)/shard_map/ppermute | solution.py:421
  74.1 3.6 %collective-permute-start.14 = (bf16[3,32,384]{2,1,0:T(8,128)(2,1)S(1)}, bf16[3,32,384]{2,1,0:T(8,128)(2,1)S(1)}, u32[]{:S(2)}, u32[]{:S(2)}) collective-permute-start(bf16[3,32,384]{2,1,0:T(8,128)(2,1)S(1)} %get-tuple-element.64), channel_id=1, source_target_pairs={{0,16},{16,32},{32,48},{48,0},{1,17},{17,33},{33,49},{49,1},{2,18}... | collective-permute-start | bytes 221192 | tf_op jit(solution)/shard_map/ppermute | solution.py:421
  75.8 4.2 %collective-permute-start.15 = (bf16[3,32,384]{2,1,0:T(8,128)(2,1)S(1)}, bf16[3,32,384]{2,1,0:T(8,128)(2,1)S(1)}, u32[]{:S(2)}, u32[]{:S(2)}) collective-permute-start(bf16[3,32,384]{2,1,0:T(8,128)(2,1)S(1)} %get-tuple-element.65), channel_id=1, source_target_pairs={{0,32},{16,48},{32,0},{48,16},{1,33},{17,49},{33,1},{49,17},{2,34}... | collective-permute-start | bytes 221192 | tf_op jit(solution)/shard_map/ppermute | solution.py:421
  75.8 4.8 %collective-permute-start.16 = (bf16[3,32,384]{2,1,0:T(8,128)(2,1)S(1)}, bf16[3,32,384]{2,1,0:T(8,128)(2,1)S(1)}, u32[]{:S(2)}, u32[]{:S(2)}) collective-permute-start(bf16[3,32,384]{2,1,0:T(8,128)(2,1)S(1)} %get-tuple-element.66), channel_id=1, source_target_pairs={{0,48},{16,0},{32,16},{48,32},{1,49},{17,1},{33,17},{49,33},{2,50}... | collective-permute-start | bytes 221192 | tf_op jit(solution)/shard_map/ppermute | solution.py:421
  81.2 14.4 %collective-permute-start.25 = (bf16[4,64,768]{2,1,0:T(8,128)(2,1)S(1)}, bf16[4,64,768]{2,1,0:T(8,128)(2,1)S(1)}, u32[]{:S(2)}, u32[]{:S(2)}) collective-permute-start(bf16[4,64,768]{2,1,0:T(8,128)(2,1)S(1)} %collective-permute-done.17.refs_0_), channel_id=1, source_target_pairs={{0,128},{64,192},{128,0},{192,64},{1,129},{65,193},{129,1},{193,65... | collective-permute-start | bytes 1179656 | tf_op jit(solution)/shard_map/ppermute | solution.py:421
  87.3 5.1 %collective-permute-start.20 = (bf16[3,32,384]{2,1,0:T(8,128)(2,1)S(1)}, bf16[3,32,384]{2,1,0:T(8,128)(2,1)S(1)}, u32[]{:S(2)}, u32[]{:S(2)}) collective-permute-start(bf16[3,32,384]{2,1,0:T(8,128)(2,1)S(1)} %add_and_cut.5), channel_id=1, source_target_pairs={{0,16},{16,32},{32,48},{48,0},{1,17},{17,33},{33,49},{49,1},{2,18}... | collective-permute-start | bytes 221192 | tf_op jit(solution)/shard_map/ppermute | solution.py:421
  87.3 6.8 %collective-permute-start.21 = (bf16[3,32,384]{2,1,0:T(8,128)(2,1)S(1)}, bf16[3,32,384]{2,1,0:T(8,128)(2,1)S(1)}, u32[]{:S(2)}, u32[]{:S(2)}) collective-permute-start(bf16[3,32,384]{2,1,0:T(8,128)(2,1)S(1)} %add_and_cut.5), channel_id=1, source_target_pairs={{0,32},{16,48},{32,0},{48,16},{1,33},{17,49},{33,1},{49,17},{2,34}... | collective-permute-start | bytes 221192 | tf_op jit(solution)/shard_map/ppermute | solution.py:421
  88.2 7.3 %collective-permute-start.22 = (bf16[3,32,384]{2,1,0:T(8,128)(2,1)S(1)}, bf16[3,32,384]{2,1,0:T(8,128)(2,1)S(1)}, u32[]{:S(2)}, u32[]{:S(2)}) collective-permute-start(bf16[3,32,384]{2,1,0:T(8,128)(2,1)S(1)} %add_and_cut.5), channel_id=1, source_target_pairs={{0,48},{16,0},{32,16},{48,32},{1,49},{17,1},{33,17},{49,33},{2,50}... | collective-permute-start | bytes 221192 | tf_op jit(solution)/shard_map/ppermute | solution.py:421
  89.3 9.0 %collective-permute-start.23 = (bf16[4,64,768]{2,1,0:T(8,128)(2,1)S(1)}, bf16[4,64,768]{2,1,0:T(8,128)(2,1)S(1)}, u32[]{:S(2)}, u32[]{:S(2)}) collective-permute-start(bf16[4,64,768]{2,1,0:T(8,128)(2,1)S(1)} %collective-permute-done.17.refs_0_), channel_id=1, source_target_pairs={{0,8},{8,0},{1,9},{9,1},{2,10},{10,2},{3,11},{11,3},{4,12},{12,4},... | collective-permute-start | bytes 1179656 | tf_op jit(solution)/shard_map/ppermute | solution.py:425
  92.5 7.9 %collective-permute-start.24 = (bf16[4,64,768]{2,1,0:T(8,128)(2,1)S(1)}, bf16[4,64,768]{2,1,0:T(8,128)(2,1)S(1)}, u32[]{:S(2)}, u32[]{:S(2)}) collective-permute-start(bf16[4,64,768]{2,1,0:T(8,128)(2,1)S(1)} %collective-permute-done.18.refs_2_), channel_id=1, source_target_pairs={{0,8},{8,0},{1,9},{9,1},{2,10},{10,2},{3,11},{11,3},{4,12},{12,4},... | collective-permute-start | bytes 1179656 | tf_op jit(solution)/shard_map/ppermute | solution.py:425
  94.1 8.3 %collective-permute-start.27 = (bf16[4,64,768]{2,1,0:T(8,128)(2,1)S(1)}, bf16[4,64,768]{2,1,0:T(8,128)(2,1)S(1)}, u32[]{:S(2)}, u32[]{:S(2)}) collective-permute-start(bf16[4,64,768]{2,1,0:T(8,128)(2,1)S(1)} %collective-permute-done.19.refs_6_), channel_id=1, source_target_pairs={{0,8},{8,0},{1,9},{9,1},{2,10},{10,2},{3,11},{11,3},{4,12},{12,4},... | collective-permute-start | bytes 1179656 | tf_op jit(solution)/shard_map/ppermute | solution.py:425
  95.6 7.7 %collective-permute-start.26 = (bf16[4,64,768]{2,1,0:T(8,128)(2,1)S(1)}, bf16[4,64,768]{2,1,0:T(8,128)(2,1)S(1)}, u32[]{:S(2)}, u32[]{:S(2)}) collective-permute-start(bf16[4,64,768]{2,1,0:T(8,128)(2,1)S(1)} %collective-permute-done.25.refs_4_), channel_id=1, source_target_pairs={{0,8},{8,0},{1,9},{9,1},{2,10},{10,2},{3,11},{11,3},{4,12},{12,4},... | collective-permute-start | bytes 1179656 | tf_op jit(solution)/shard_map/ppermute | solution.py:425
  97.4 20.3 %collective-permute-start.33 = (bf16[4,3,32,384]{3,2,1,0:T(8,128)(2,1)S(1)}, bf16[4,3,32,384]{3,2,1,0:T(8,128)(2,1)S(1)}, u32[]{:S(2)}, u32[]{:S(2)}) collective-permute-start(bf16[4,3,32,384]{3,2,1,0:T(8,128)(2,1)S(1)} %pad_maximum_fusion.refs_0_), channel_id=1, source_target_pairs={{0,192},{64,0},{128,64},{192,128},{1,193},{65,1},{129,65},{193,129... | collective-permute-start | bytes 884744 | tf_op jit(solution)/shard_map/ppermute | solution.py:421
  98.3 19.3 %collective-permute-start.31 = (bf16[4,3,32,384]{3,2,1,0:T(8,128)(2,1)S(1)}, bf16[4,3,32,384]{3,2,1,0:T(8,128)(2,1)S(1)}, u32[]{:S(2)}, u32[]{:S(2)}) collective-permute-start(bf16[4,3,32,384]{3,2,1,0:T(8,128)(2,1)S(1)} %pad_maximum_fusion.refs_0_), channel_id=1, source_target_pairs={{0,128},{64,192},{128,0},{192,64},{1,129},{65,193},{129,1},{193,65... | collective-permute-start | bytes 884744 | tf_op jit(solution)/shard_map/ppermute | solution.py:421
  100.4 17.8 %collective-permute-start.29 = (bf16[4,3,32,384]{3,2,1,0:T(8,128)(2,1)S(1)}, bf16[4,3,32,384]{3,2,1,0:T(8,128)(2,1)S(1)}, u32[]{:S(2)}, u32[]{:S(2)}) collective-permute-start(bf16[4,3,32,384]{3,2,1,0:T(8,128)(2,1)S(1)} %pad_maximum_fusion.refs_0_), channel_id=1, source_target_pairs={{0,64},{64,128},{128,192},{192,0},{1,65},{65,129},{129,193},{193,1... | collective-permute-start | bytes 884744 | tf_op jit(solution)/shard_map/ppermute | solution.py:421
  102.4 15.8 %collective-permute-start.28 = (bf16[4,3,32,384]{3,2,1,0:T(8,128)(2,1)S(1)}, bf16[4,3,32,384]{3,2,1,0:T(8,128)(2,1)S(1)}, u32[]{:S(2)}, u32[]{:S(2)}) collective-permute-start(bf16[4,3,32,384]{3,2,1,0:T(8,128)(2,1)S(1)} %pad_maximum_fusion.refs_0_), channel_id=1, source_target_pairs={{0,8},{8,0},{1,9},{9,1},{2,10},{10,2},{3,11},{11,3},{4,12},{12,4},... | collective-permute-start | bytes 884744 | tf_op jit(solution)/shard_map/ppermute | solution.py:425
  (16 other events, 46.5 us)
where the time goes:
time: 123 us; the launch traced here: 122 us
  starting transfers between devices  58.8 us (48%)
  Pallas kernels  34.2 us (28%)
  waiting for transfers between devices  22.8 us (19%)
  local copies, waits for them, and re-layouts  5.58 us (5%)
    ppermute x14, starting transfers between devices, swap(): return lax.ppermute(x, axis, [(0, 1), (1, 0)])  30.2 us
    pallas_call x10, Pallas kernels, call(): pl.pallas_call(kernel, in_specs=[pl.BlockSpec(memory_space=pltpu.SMEM)] +...  29.8 us
    ppermute x21, starting transfers between devices, shift(): return lax.ppermute(x, axis, [(i, (i + d) % 4) for i in range(4)])  28.7 us
    ppermute x14, waiting for transfers between devices, swap(): return lax.ppermute(x, axis, [(0, 1), (1, 0)])  15.8 us
    ppermute x21, waiting for transfers between devices, shift(): return lax.ppermute(x, axis, [(i, (i + d) % 4) for i in range(4)])  7.01 us
    unnamed x26, local copies, waits for them, and re-layouts  5.26 us
  transfers between devices with their start and end apart: 35, of which 9 were waited for; matrix products, arithmetic and copies ran while one was open for 0% of the time, Pallas kernels for 24%

commit v1 on v0

--- a/solution.py
+++ b/solution.py
@@ -90,6 +90,11 @@
 
 
 def each_head(body, together):
+    if together == NH:
+        for u in range(NH):
+            body(u, u)
+        return
+
     @pl.loop(0, NH // together)
     def _(p):
         for u in range(together):
@@ -102,6 +107,8 @@
 
 
 def head_cols(g, r):
+    if isinstance(g, int) and isinstance(r, int):
+        return slice(g * WIDE + r * DH, g * WIDE + (r + 1) * DH)
     return pl.ds(pl.multiple_of(g * WIDE + r * DH, DH), DH)
 
 
@@ -151,7 +158,7 @@
                 held[h, 1:2, out] = total
                 held[h, 2:3, out] = part
 
-        each_head(head, 3)
+        each_head(head, NH)
 
     each_chunk(scal, half, chunk)
     store_rows(stat, held)
@@ -189,7 +196,7 @@
                 held[h, 1:2, cols] = total
                 held[h, 2:3, cols] = part
 
-        each_head(head, 3)
+        each_head(head, NH)
 
     each_chunk(scal, half, chunk)
     store_rows(stat, held)
@@ -261,7 +268,7 @@
 
 def own_head(scal, at):
     h = lax.rem(scal[S_CORE] * HALF + at, NH)
-    return h, head_cols(0, h), at // HALF, head_cols(0, lax.rem(at, HALF))
+    return h, head_cols(0, h), at // HALF, head_cols(0, at % HALF if isinstance(at, int) else lax.rem(at, HALF))
 
 
 def own_video_kernel(scal, vq, vg, ak, av, vstat, keep, send, dvq, prob, dscore, acc, sums):
@@ -279,7 +286,7 @@
             sums[step, 1, rows, sc] = dot_nn(prob[u], vg[:, hc]).astype(BF16)
             acc[at] += dot_nn(ak[rows, hc].T, ds)
 
-        each_head(head, 3)
+        each_head(head, NH)
 
     def idle(rows):
         for step in range(2):
@@ -311,7 +318,7 @@
             dvk[:, hc] += dot_nn(ds, aq[rows, hc])
             dvv[:, hc] += dot_nn(prob[u], ag[rows, hc])
 
-        each_head(head, 3)
+        each_head(head, NH)
 
     def idle(rows):
         for step in range(2):
@@ -327,7 +334,7 @@
 
 def own_video(scal, vq, vg, ak, av, vstat):
     part = ((2, ROWS, WIDE), BF16)
-    scratch = [pltpu.VMEM((3, CH, ROWS), BF16)] * 2 + [pltpu.VMEM((NH, DH, ROWS), F32)]
+    scratch = [pltpu.VMEM((NH, CH, ROWS), BF16)] * 2 + [pltpu.VMEM((NH, DH, ROWS), F32)]
     scratch += [pltpu.VMEM((2, 2, ROWS, WIDE), BF16)]
     return call(
         own_video_kernel, 5, [part, part, (MINE, F32)], scratch, 28, 20, "own_video",
@@ -337,7 +344,7 @@
 
 def own_audio(scal, vk, vv, aq, ag, astat):
     part = ((1, ROWS, WIDE), BF16)
-    scratch = [pltpu.VMEM((3, ROWS, CH), BF16)] * 2 + [pltpu.VMEM((2, 1, ROWS, WIDE), BF16)]
+    scratch = [pltpu.VMEM((NH, ROWS, CH), BF16)] * 2 + [pltpu.VMEM((2, 1, ROWS, WIDE), BF16)]
     return call(
         own_audio_kernel, 5, [part, part, (MINE, F32), (MINE, F32)], scratch, 28, 20, "own_audio",
         scal, vk, vv, aq, ag, astat,

time: 123 us -> 121 us (0.984)
  the two profiles are of different devices: /device:TPU:55 before, /device:TPU:4 now
where the time goes in v1:
time: 121 us; the launch traced here: 118 us
  starting transfers between devices  45.1 us (37%)
  waiting for transfers between devices  42.8 us (35%)
  Pallas kernels  23.5 us (19%)
  local copies, waits for them, and re-layouts  6.03 us (5%)
    ppermute x21, starting transfers between devices, shift(): return lax.ppermute(x, axis, [(i, (i + d) % 4) for i in range(4)])  38.3 us
    ppermute x21, waiting for transfers between devices, shift(): return lax.ppermute(x, axis, [(i, (i + d) % 4) for i in range(4)])  22.5 us
    ppermute x14, waiting for transfers between devices, swap(): return lax.ppermute(x, axis, [(0, 1), (1, 0)])  20.3 us
    pallas_call x10, Pallas kernels, call(): pl.pallas_call(kernel, in_specs=[pl.BlockSpec(memory_space=pltpu.SMEM)] +...  19.1 us
    ppermute x14, starting transfers between devices, swap(): return lax.ppermute(x, axis, [(0, 1), (1, 0)])  6.77 us
    unnamed x26, local copies, waits for them, and re-layouts  5.71 us
  transfers between devices with their start and end apart: 35, of which 14 were waited for; matrix products, arithmetic and copies ran while one was open for 0% of the time, Pallas kernels for 16%

profile of v1, /device:TPU:4, one launch (start us, length us, event | category | flops | bytes accessed | tf_op | source)
XLA Modules:
  0.0 118.4 jit_solution(2140740664707632517)
XLA Ops:
  6.2 1.9 %audio_stats.1 = (f32[3,8,512]{2,1,0:T(8,128)S(1)}, bf16[2,64,768]{2,1,0:T(8,128)(2,1)S(1)}) custom-call(s32[68]{0:T(128)S(1)} %concatenate.3.scal, bf16[512,768]{1,0:T(8,128)(2,1)S(1)} %copy-done.9, bf16[512,768]{1,0:T(8,128)(2,1)S(1)} %copy-done.11, bf16[512,768]{1,0:T(8,128)(2,1)S(1)} %copy-done.3, bf16[512,768]{1,0:T(8,128)(2,1)S(1)} %copy-done.5), custom_call_target="tpu_custom_call" | custom-call | flops 20000000000 | bytes 100000 | tf_op jit(solution)/shard_map/audio_stats/pallas_call | solution.py:45
  8.3 2.1 %video_stats.1 = (f32[3,8,512]{2,1,0:T(8,128)S(1)}, bf16[4,64,768]{2,1,0:T(8,128)(2,1)S(1)}) custom-call(s32[68]{0:T(128)S(1)} %concatenate.3.scal, bf16[512,768]{1,0:T(8,128)(2,1)S(1)} %copy-done.7, bf16[512,768]{1,0:T(8,128)(2,1)S(1)} %copy-done.8, bf16[512,768]{1,0:T(8,128)(2,1)S(1)} %copy-done.1, bf16[512,768]{1,0:T(8,128)(2,1)S(1)} %copy-done.2, ...), custom_call_target="tpu_custom_call" | custom-call | flops 20000000000 | bytes 100000 | tf_op jit(solution)/shard_map/video_stats/pallas_call | solution.py:45
  10.4 5.5 %collective-permute-start.4 = (f32[3,8,512]{2,1,0:T(8,128)S(1)}, f32[3,8,512]{2,1,0:T(8,128)S(1)}, u32[]{:S(2)}, u32[]{:S(2)}) collective-permute-start(f32[3,8,512]{2,1,0:T(8,128)S(1)} %get-tuple-element.49.refs_0_), channel_id=1, source_target_pairs={{0,4},{4,0},{1,5},{5,1},{2,6},{6,2},{3,7},{7,3},{8,12},{12,8},{9,1... | collective-permute-start | bytes 147464 | tf_op jit(solution)/shard_map/ppermute | solution.py:432
  17.6 1.6 %collective-permute-start.2 = (f32[3,8,512]{2,1,0:T(8,128)S(1)}, f32[3,8,512]{2,1,0:T(8,128)S(1)}, u32[]{:S(2)}, u32[]{:S(2)}) collective-permute-start(f32[3,8,512]{2,1,0:T(8,128)S(1)} %merge.4.refs_0_), channel_id=1, source_target_pairs={{0,32},{16,48},{32,0},{48,16},{1,33},{17,49},{33,1},{49,17},{2,34}... | collective-permute-start | bytes 147464 | tf_op jit(solution)/shard_map/ppermute | solution.py:428
  19.2 1.8 %collective-permute-start.3 = (f32[3,8,512]{2,1,0:T(8,128)S(1)}, f32[3,8,512]{2,1,0:T(8,128)S(1)}, u32[]{:S(2)}, u32[]{:S(2)}) collective-permute-start(f32[3,8,512]{2,1,0:T(8,128)S(1)} %merge.4.refs_0_), channel_id=1, source_target_pairs={{0,48},{16,0},{32,16},{48,32},{1,49},{17,1},{33,17},{49,33},{2,50}... | collective-permute-start | bytes 147464 | tf_op jit(solution)/shard_map/ppermute | solution.py:428
  21.6 2.3 %collective-permute-done.1.refs_1_ = f32[3,8,512]{2,1,0:T(8,128)S(1)} collective-permute-done((f32[3,8,512]{2,1,0:T(8,128)S(1)}, f32[3,8,512]{2,1,0:T(8,128)S(1)}, u32[]{:S(2)}, u32[]{:S(2)}) %collective-permute-start.1) | collective-permute-done | bytes 49184 | tf_op jit(solution)/shard_map/ppermute | solution.py:428
  25.5 2.8 %collective-permute-start.6 = (f32[3,8,512]{2,1,0:T(8,128)S(1)}, f32[3,8,512]{2,1,0:T(8,128)S(1)}, u32[]{:S(2)}, u32[]{:S(2)}) collective-permute-start(f32[3,8,512]{2,1,0:T(8,128)S(1)} %merge.5.refs_0_), channel_id=1, source_target_pairs={{0,64},{64,128},{128,192},{192,0},{1,65},{65,129},{129,193},{193,1... | collective-permute-start | bytes 147464 | tf_op jit(solution)/shard_map/ppermute | solution.py:428
  28.3 5.8 %collective-permute-start.7 = (f32[3,8,512]{2,1,0:T(8,128)S(1)}, f32[3,8,512]{2,1,0:T(8,128)S(1)}, u32[]{:S(2)}, u32[]{:S(2)}) collective-permute-start(f32[3,8,512]{2,1,0:T(8,128)S(1)} %merge.5.refs_0_), channel_id=1, source_target_pairs={{0,128},{64,192},{128,0},{192,64},{1,129},{65,193},{129,1},{193,65... | collective-permute-start | bytes 147464 | tf_op jit(solution)/shard_map/ppermute | solution.py:428
  34.7 4.3 %own_video.1 = (bf16[2,512,384]{2,1,0:T(8,128)(2,1)S(1)}, bf16[2,512,384]{2,1,0:T(8,128)(2,1)S(1)}, f32[512,768]{1,0:T(8,128)S(1)}) custom-call(s32[68]{0:T(128)S(1)} %concatenate.3.scal, bf16[512,768]{1,0:T(8,128)(2,1)S(1)} %copy-done.7, bf16[512,768]{1,0:T(8,128)(2,1)S(1)} %copy-done.8, bf16[512,768]{1,0:T(8,128)(2,1)S(1)} %copy-done.1, ...), custom_call_target="tpu_custom_call" | custom-call | flops 20000000000 | bytes 100000 | tf_op jit(solution)/shard_map/own_video/pallas_call | solution.py:45
  40.9 4.0 %own_audio.1 = (bf16[1,512,384]{2,1,0:T(8,128)(2,1)S(1)}, bf16[1,512,384]{2,1,0:T(8,128)(2,1)S(1)}, f32[512,768]{1,0:T(8,128)S(1)}, f32[512,768]{1,0:T(8,128)S(1)}) custom-call(s32[68]{0:T(128)S(1)} %concatenate.3.scal, bf16[512,768]{1,0:T(8,128)(2,1)S(1)} %copy-done.10, bf16[512,768]{1,0:T(8,128)(2,1)S(1)} %copy-done.12, bf16[512,768]{1,0:T(8,128)(2,1)S(1)} %copy-done.4, ...), custom_call_target="tpu_custom_call" | custom-call | flops 20000000000 | bytes 100000 | tf_op jit(solution)/shard_map/own_audio/pallas_call | solution.py:45
  44.8 3.0 %collective-permute-done.9.astat = f32[2,8,512]{2,1,0:T(8,128)S(1)} collective-permute-done((f32[2,8,512]{2,1,0:T(8,128)S(1)}, f32[2,8,512]{2,1,0:T(8,128)S(1)}, u32[]{:S(2)}, u32[]{:S(2)}) %collective-permute-start.9) | collective-permute-done | bytes 32800 | tf_op jit(solution)/shard_map/ppermute | solution.py:432
  48.2 1.3 %collective-permute-done.10.refs_3_ = bf16[1,512,384]{2,1,0:T(8,128)(2,1)S(1)} collective-permute-done((bf16[1,512,384]{2,1,0:T(8,128)(2,1)S(1)}, bf16[1,512,384]{2,1,0:T(8,128)(2,1)S(1)}, u32[]{:S(2)}, u32[]{:S(2)}) %collective-permute-start.10) | collective-permute-done | bytes 393248 | tf_op jit(solution)/shard_map/ppermute | solution.py:432
  50.4 4.2 %collective-permute-start.11 = (bf16[3,128,384]{2,1,0:T(8,128)(2,1)S(1)}, bf16[3,128,384]{2,1,0:T(8,128)(2,1)S(1)}, u32[]{:S(2)}, u32[]{:S(2)}) collective-permute-start(bf16[3,128,384]{2,1,0:T(8,128)(2,1)S(1)} %get-tuple-element.60), channel_id=1, source_target_pairs={{0,64},{64,128},{128,192},{192,0},{1,65},{65,129},{129,193},{193,1... | collective-permute-start | bytes 884744 | tf_op jit(solution)/shard_map/ppermute | solution.py:428
  54.6 1.8 %collective-permute-start.12 = (bf16[3,128,384]{2,1,0:T(8,128)(2,1)S(1)}, bf16[3,128,384]{2,1,0:T(8,128)(2,1)S(1)}, u32[]{:S(2)}, u32[]{:S(2)}) collective-permute-start(bf16[3,128,384]{2,1,0:T(8,128)(2,1)S(1)} %get-tuple-element.61), channel_id=1, source_target_pairs={{0,128},{64,192},{128,0},{192,64},{1,129},{65,193},{129,1},{193,65... | collective-permute-start | bytes 884744 | tf_op jit(solution)/shard_map/ppermute | solution.py:428
  57.4 14.4 %collective-permute-done.17.refs_0_ = bf16[4,64,768]{2,1,0:T(8,128)(2,1)S(1)} collective-permute-done((bf16[4,64,768]{2,1,0:T(8,128)(2,1)S(1)}, bf16[4,64,768]{2,1,0:T(8,128)(2,1)S(1)}, u32[]{:S(2)}, u32[]{:S(2)}) %collective-permute-start.17) | collective-permute-done | bytes 393248 | tf_op jit(solution)/shard_map/ppermute | solution.py:432
  71.7 3.1 %collective-permute-start.18 = (bf16[4,64,768]{2,1,0:T(8,128)(2,1)S(1)}, bf16[4,64,768]{2,1,0:T(8,128)(2,1)S(1)}, u32[]{:S(2)}, u32[]{:S(2)}) collective-permute-start(bf16[4,64,768]{2,1,0:T(8,128)(2,1)S(1)} %collective-permute-done.17.refs_0_), channel_id=1, source_target_pairs={{0,64},{64,128},{128,192},{192,0},{1,65},{65,129},{129,193},{193,1... | collective-permute-start | bytes 1179656 | tf_op jit(solution)/shard_map/ppermute | solution.py:428
  75.7 3.8 %collective-permute-start.14 = (bf16[3,32,384]{2,1,0:T(8,128)(2,1)S(1)}, bf16[3,32,384]{2,1,0:T(8,128)(2,1)S(1)}, u32[]{:S(2)}, u32[]{:S(2)}) collective-permute-start(bf16[3,32,384]{2,1,0:T(8,128)(2,1)S(1)} %get-tuple-element.64), channel_id=1, source_target_pairs={{0,16},{16,32},{32,48},{48,0},{1,17},{17,33},{33,49},{49,1},{2,18}... | collective-permute-start | bytes 221192 | tf_op jit(solution)/shard_map/ppermute | solution.py:428
  80.2 1.8 %collective-permute-start.16 = (bf16[3,32,384]{2,1,0:T(8,128)(2,1)S(1)}, bf16[3,32,384]{2,1,0:T(8,128)(2,1)S(1)}, u32[]{:S(2)}, u32[]{:S(2)}) collective-permute-start(bf16[3,32,384]{2,1,0:T(8,128)(2,1)S(1)} %get-tuple-element.66), channel_id=1, source_target_pairs={{0,48},{16,0},{32,16},{48,32},{1,49},{17,1},{33,17},{49,33},{2,50}... | collective-permute-start | bytes 221192 | tf_op jit(solution)/shard_map/ppermute | solution.py:428
  82.5 3.4 %collective-permute-done.15.refs_2_ = bf16[3,32,384]{2,1,0:T(8,128)(2,1)S(1)} collective-permute-done((bf16[3,32,384]{2,1,0:T(8,128)(2,1)S(1)}, bf16[3,32,384]{2,1,0:T(8,128)(2,1)S(1)}, u32[]{:S(2)}, u32[]{:S(2)}) %collective-permute-start.15) | collective-permute-done | bytes 73760 | tf_op jit(solution)/shard_map/ppermute | solution.py:428
  86.9 1.4 %collective-permute-start.20 = (bf16[3,32,384]{2,1,0:T(8,128)(2,1)S(1)}, bf16[3,32,384]{2,1,0:T(8,128)(2,1)S(1)}, u32[]{:S(2)}, u32[]{:S(2)}) collective-permute-start(bf16[3,32,384]{2,1,0:T(8,128)(2,1)S(1)} %add_and_cut.5), channel_id=1, source_target_pairs={{0,16},{16,32},{32,48},{48,0},{1,17},{17,33},{33,49},{49,1},{2,18}... | collective-permute-start | bytes 221192 | tf_op jit(solution)/shard_map/ppermute | solution.py:428
  89.6 1.4 %collective-permute-start.22 = (bf16[3,32,384]{2,1,0:T(8,128)(2,1)S(1)}, bf16[3,32,384]{2,1,0:T(8,128)(2,1)S(1)}, u32[]{:S(2)}, u32[]{:S(2)}) collective-permute-start(bf16[3,32,384]{2,1,0:T(8,128)(2,1)S(1)} %add_and_cut.5), channel_id=1, source_target_pairs={{0,48},{16,0},{32,16},{48,32},{1,49},{17,1},{33,17},{49,33},{2,50}... | collective-permute-start | bytes 221192 | tf_op jit(solution)/shard_map/ppermute | solution.py:428
  90.9 2.4 %collective-permute-done.20 = bf16[3,32,384]{2,1,0:T(8,128)(2,1)S(1)} collective-permute-done((bf16[3,32,384]{2,1,0:T(8,128)(2,1)S(1)}, bf16[3,32,384]{2,1,0:T(8,128)(2,1)S(1)}, u32[]{:S(2)}, u32[]{:S(2)}) %collective-permute-start.20) | collective-permute-done | bytes 73760 | tf_op jit(solution)/shard_map/ppermute | solution.py:428
  93.4 1.9 %collective-permute-done.21 = bf16[3,32,384]{2,1,0:T(8,128)(2,1)S(1)} collective-permute-done((bf16[3,32,384]{2,1,0:T(8,128)(2,1)S(1)}, bf16[3,32,384]{2,1,0:T(8,128)(2,1)S(1)}, u32[]{:S(2)}, u32[]{:S(2)}) %collective-permute-start.21) | collective-permute-done | bytes 73760 | tf_op jit(solution)/shard_map/ppermute | solution.py:428
  96.6 1.5 %collective-permute-start.33 = (bf16[4,3,32,384]{3,2,1,0:T(8,128)(2,1)S(1)}, bf16[4,3,32,384]{3,2,1,0:T(8,128)(2,1)S(1)}, u32[]{:S(2)}, u32[]{:S(2)}) collective-permute-start(bf16[4,3,32,384]{3,2,1,0:T(8,128)(2,1)S(1)} %pad_maximum_fusion.refs_0_), channel_id=1, source_target_pairs={{0,192},{64,0},{128,64},{192,128},{1,193},{65,1},{129,65},{193,129... | collective-permute-start | bytes 884744 | tf_op jit(solution)/shard_map/ppermute | solution.py:428
  98.9 1.4 %collective-permute-start.29 = (bf16[4,3,32,384]{3,2,1,0:T(8,128)(2,1)S(1)}, bf16[4,3,32,384]{3,2,1,0:T(8,128)(2,1)S(1)}, u32[]{:S(2)}, u32[]{:S(2)}) collective-permute-start(bf16[4,3,32,384]{3,2,1,0:T(8,128)(2,1)S(1)} %pad_maximum_fusion.refs_0_), channel_id=1, source_target_pairs={{0,64},{64,128},{128,192},{192,0},{1,65},{65,129},{129,193},{193,1... | collective-permute-start | bytes 884744 | tf_op jit(solution)/shard_map/ppermute | solution.py:428
  100.3 2.5 %other_video.1 = bf16[512,768]{1,0:T(8,128)(2,1)} custom-call(s32[68]{0:T(128)S(1)} %concatenate.3.scal, bf16[512,768]{1,0:T(8,128)(2,1)S(1)} %copy-done.7, bf16[512,768]{1,0:T(8,128)(2,1)S(1)} %copy-done.8, f32[2,8,512]{2,1,0:T(8,128)S(1)} %merge.6.vstat, f32[512,768]{1,0:T(8,128)S(1)} %get-tuple-element.54.pvq, ...), custom_call_target="tpu_custom_call" | custom-call | flops 20000000000 | bytes 100000 | tf_op jit(solution)/shard_map/other_video/pallas_call | solution.py:45
  102.8 2.1 %other_audio.1 = (bf16[512,768]{1,0:T(8,128)(2,1)}, bf16[512,768]{1,0:T(8,128)(2,1)}) custom-call(s32[68]{0:T(128)S(1)} %concatenate.3.scal, bf16[512,768]{1,0:T(8,128)(2,1)S(1)} %copy-done.10, bf16[512,768]{1,0:T(8,128)(2,1)S(1)} %copy-done.12, f32[2,8,512]{2,1,0:T(8,128)S(1)} %collective-permute-done.9.astat, f32[512,768]{1,0:T(8,128)S(1)} %get-tuple-element.69.pvk, ...), custom_call_target="tpu_custom_call" | custom-call | flops 20000000000 | bytes 100000 | tf_op jit(solution)/shard_map/other_audio/pallas_call | solution.py:45
  104.9 1.5 %collective-permute-done.33.refs_6_ = bf16[4,3,32,384]{3,2,1,0:T(8,128)(2,1)S(1)} collective-permute-done((bf16[4,3,32,384]{3,2,1,0:T(8,128)(2,1)S(1)}, bf16[4,3,32,384]{3,2,1,0:T(8,128)(2,1)S(1)}, u32[]{:S(2)}, u32[]{:S(2)}) %collective-permute-start.33) | collective-permute-done | bytes 294944 | tf_op jit(solution)/shard_map/ppermute | solution.py:428
  106.4 3.1 %collective-permute-done.31.refs_4_ = bf16[4,3,32,384]{3,2,1,0:T(8,128)(2,1)S(1)} collective-permute-done((bf16[4,3,32,384]{3,2,1,0:T(8,128)(2,1)S(1)}, bf16[4,3,32,384]{3,2,1,0:T(8,128)(2,1)S(1)}, u32[]{:S(2)}, u32[]{:S(2)}) %collective-permute-start.31) | collective-permute-done | bytes 294944 | tf_op jit(solution)/shard_map/ppermute | solution.py:428
  109.5 5.1 %collective-permute-done.29.refs_2_ = bf16[4,3,32,384]{3,2,1,0:T(8,128)(2,1)S(1)} collective-permute-done((bf16[4,3,32,384]{3,2,1,0:T(8,128)(2,1)S(1)}, bf16[4,3,32,384]{3,2,1,0:T(8,128)(2,1)S(1)}, u32[]{:S(2)}, u32[]{:S(2)}) %collective-permute-start.29) | collective-permute-done | bytes 294944 | tf_op jit(solution)/shard_map/ppermute | solution.py:428
  114.6 1.6 %collective-permute-done.30.refs_3_ = bf16[4,3,32,384]{3,2,1,0:T(8,128)(2,1)S(1)} collective-permute-done((bf16[4,3,32,384]{3,2,1,0:T(8,128)(2,1)S(1)}, bf16[4,3,32,384]{3,2,1,0:T(8,128)(2,1)S(1)}, u32[]{:S(2)}, u32[]{:S(2)}) %collective-permute-start.30) | collective-permute-done | bytes 294944 | tf_op jit(solution)/shard_map/ppermute | solution.py:432
  116.2 2.2 %place.1 = (bf16[512,768]{1,0:T(8,128)(2,1)}, bf16[512,768]{1,0:T(8,128)(2,1)}, bf16[512,768]{1,0:T(8,128)(2,1)}) custom-call(s32[68]{0:T(128)S(1)} %concatenate.3.scal, bf16[4,3,32,384]{3,2,1,0:T(8,128)(2,1)S(1)} %pad_maximum_fusion.refs_0_, bf16[4,3,32,384]{3,2,1,0:T(8,128)(2,1)S(1)} %collective-permute-done.28.refs_1_, ...), custom_call_target="tpu_custom_call" | custom-call | flops 1000000000 | bytes 100000 | tf_op jit(solution)/shard_map/place/pallas_call | solution.py:504
  (83 shorter events, 20.5 us)
Async XLA Ops:
  8.2 7.8 %collective-permute-start = (f32[3,8,512]{2,1,0:T(8,128)S(1)}, f32[3,8,512]{2,1,0:T(8,128)S(1)}, u32[]{:S(2)}, u32[]{:S(2)}) collective-permute-start(f32[3,8,512]{2,1,0:T(8,128)S(1)} %get-tuple-element.50.refs_0_), channel_id=1, source_target_pairs={{0,8},{8,0},{1,9},{9,1},{2,10},{10,2},{3,11},{11,3},{4,12},{12,4},... | collective-permute-start | bytes 147464 | tf_op jit(solution)/shard_map/ppermute | solution.py:432
  10.4 10.6 %collective-permute-start.4 = (f32[3,8,512]{2,1,0:T(8,128)S(1)}, f32[3,8,512]{2,1,0:T(8,128)S(1)}, u32[]{:S(2)}, u32[]{:S(2)}) collective-permute-start(f32[3,8,512]{2,1,0:T(8,128)S(1)} %get-tuple-element.49.refs_0_), channel_id=1, source_target_pairs={{0,4},{4,0},{1,5},{5,1},{2,6},{6,2},{3,7},{7,3},{8,12},{12,8},{9,1... | collective-permute-start | bytes 147464 | tf_op jit(solution)/shard_map/ppermute | solution.py:432
  16.5 7.3 %collective-permute-start.1 = (f32[3,8,512]{2,1,0:T(8,128)S(1)}, f32[3,8,512]{2,1,0:T(8,128)S(1)}, u32[]{:S(2)}, u32[]{:S(2)}) collective-permute-start(f32[3,8,512]{2,1,0:T(8,128)S(1)} %merge.4.refs_0_), channel_id=1, source_target_pairs={{0,16},{16,32},{32,48},{48,0},{1,17},{17,33},{33,49},{49,1},{2,18}... | collective-permute-start | bytes 147464 | tf_op jit(solution)/shard_map/ppermute | solution.py:428
  17.6 7.3 %collective-permute-start.2 = (f32[3,8,512]{2,1,0:T(8,128)S(1)}, f32[3,8,512]{2,1,0:T(8,128)S(1)}, u32[]{:S(2)}, u32[]{:S(2)}) collective-permute-start(f32[3,8,512]{2,1,0:T(8,128)S(1)} %merge.4.refs_0_), channel_id=1, source_target_pairs={{0,32},{16,48},{32,0},{48,16},{1,33},{17,49},{33,1},{49,17},{2,34}... | collective-permute-start | bytes 147464 | tf_op jit(solution)/shard_map/ppermute | solution.py:428
  19.2 5.7 %collective-permute-start.3 = (f32[3,8,512]{2,1,0:T(8,128)S(1)}, f32[3,8,512]{2,1,0:T(8,128)S(1)}, u32[]{:S(2)}, u32[]{:S(2)}) collective-permute-start(f32[3,8,512]{2,1,0:T(8,128)S(1)} %merge.4.refs_0_), channel_id=1, source_target_pairs={{0,48},{16,0},{32,16},{48,32},{1,49},{17,1},{33,17},{49,33},{2,50}... | collective-permute-start | bytes 147464 | tf_op jit(solution)/shard_map/ppermute | solution.py:428
  25.5 13.7 %collective-permute-start.6 = (f32[3,8,512]{2,1,0:T(8,128)S(1)}, f32[3,8,512]{2,1,0:T(8,128)S(1)}, u32[]{:S(2)}, u32[]{:S(2)}) collective-permute-start(f32[3,8,512]{2,1,0:T(8,128)S(1)} %merge.5.refs_0_), channel_id=1, source_target_pairs={{0,64},{64,128},{128,192},{192,0},{1,65},{65,129},{129,193},{193,1... | collective-permute-start | bytes 147464 | tf_op jit(solution)/shard_map/ppermute | solution.py:428
  28.3 10.9 %collective-permute-start.7 = (f32[3,8,512]{2,1,0:T(8,128)S(1)}, f32[3,8,512]{2,1,0:T(8,128)S(1)}, u32[]{:S(2)}, u32[]{:S(2)}) collective-permute-start(f32[3,8,512]{2,1,0:T(8,128)S(1)} %merge.5.refs_0_), channel_id=1, source_target_pairs={{0,128},{64,192},{128,0},{192,64},{1,129},{65,193},{129,1},{193,65... | collective-permute-start | bytes 147464 | tf_op jit(solution)/shard_map/ppermute | solution.py:428
  34.1 5.1 %collective-permute-start.8 = (f32[3,8,512]{2,1,0:T(8,128)S(1)}, f32[3,8,512]{2,1,0:T(8,128)S(1)}, u32[]{:S(2)}, u32[]{:S(2)}) collective-permute-start(f32[3,8,512]{2,1,0:T(8,128)S(1)} %merge.5.refs_0_), channel_id=1, source_target_pairs={{0,192},{64,0},{128,64},{192,128},{1,193},{65,1},{129,65},{193,129... | collective-permute-start | bytes 147464 | tf_op jit(solution)/shard_map/ppermute | solution.py:428
  39.1 10.5 %collective-permute-start.5 = (bf16[2,512,384]{2,1,0:T(8,128)(2,1)S(1)}, bf16[2,512,384]{2,1,0:T(8,128)(2,1)S(1)}, u32[]{:S(2)}, u32[]{:S(2)}) collective-permute-start(bf16[2,512,384]{2,1,0:T(8,128)(2,1)S(1)} %get-tuple-element.53), channel_id=1, source_target_pairs={{0,8},{8,0},{1,9},{9,1},{2,10},{10,2},{3,11},{11,3},{4,12},{12,4},... | collective-permute-start | bytes 2359304 | tf_op jit(solution)/shard_map/ppermute | solution.py:432
  39.8 8.1 %collective-permute-start.9 = (f32[2,8,512]{2,1,0:T(8,128)S(1)}, f32[2,8,512]{2,1,0:T(8,128)S(1)}, u32[]{:S(2)}, u32[]{:S(2)}) collective-permute-start(f32[2,8,512]{2,1,0:T(8,128)S(1)} %merge.7.astat), channel_id=1, source_target_pairs={{0,4},{4,0},{1,5},{5,1},{2,6},{6,2},{3,7},{7,3},{8,12},{12,8},{9,1... | collective-permute-start | bytes 98312 | tf_op jit(solution)/shard_map/ppermute | solution.py:432
  47.9 23.9 %collective-permute-start.17 = (bf16[4,64,768]{2,1,0:T(8,128)(2,1)S(1)}, bf16[4,64,768]{2,1,0:T(8,128)(2,1)S(1)}, u32[]{:S(2)}, u32[]{:S(2)}) collective-permute-start(bf16[4,64,768]{2,1,0:T(8,128)(2,1)S(1)} %get-tuple-element.68), channel_id=1, source_target_pairs={{0,4},{4,0},{1,5},{5,1},{2,6},{6,2},{3,7},{7,3},{8,12},{12,8},{9,1... | collective-permute-start | bytes 1179656 | tf_op jit(solution)/shard_map/ppermute | solution.py:432
  50.4 21.3 %collective-permute-start.11 = (bf16[3,128,384]{2,1,0:T(8,128)(2,1)S(1)}, bf16[3,128,384]{2,1,0:T(8,128)(2,1)S(1)}, u32[]{:S(2)}, u32[]{:S(2)}) collective-permute-start(bf16[3,128,384]{2,1,0:T(8,128)(2,1)S(1)} %get-tuple-element.60), channel_id=1, source_target_pairs={{0,64},{64,128},{128,192},{192,0},{1,65},{65,129},{129,193},{193,1... | collective-permute-start | bytes 884744 | tf_op jit(solution)/shard_map/ppermute | solution.py:428
  54.6 20.4 %collective-permute-start.12 = (bf16[3,128,384]{2,1,0:T(8,128)(2,1)S(1)}, bf16[3,128,384]{2,1,0:T(8,128)(2,1)S(1)}, u32[]{:S(2)}, u32[]{:S(2)}) collective-permute-start(bf16[3,128,384]{2,1,0:T(8,128)(2,1)S(1)} %get-tuple-element.61), channel_id=1, source_target_pairs={{0,128},{64,192},{128,0},{192,64},{1,129},{65,193},{129,1},{193,65... | collective-permute-start | bytes 884744 | tf_op jit(solution)/shard_map/ppermute | solution.py:428
  56.4 18.6 %collective-permute-start.13 = (bf16[3,128,384]{2,1,0:T(8,128)(2,1)S(1)}, bf16[3,128,384]{2,1,0:T(8,128)(2,1)S(1)}, u32[]{:S(2)}, u32[]{:S(2)}) collective-permute-start(bf16[3,128,384]{2,1,0:T(8,128)(2,1)S(1)} %get-tuple-element.62), channel_id=1, source_target_pairs={{0,192},{64,0},{128,64},{192,128},{1,193},{65,1},{129,65},{193,129... | collective-permute-start | bytes 884744 | tf_op jit(solution)/shard_map/ppermute | solution.py:428
  71.7 15.1 %collective-permute-start.18 = (bf16[4,64,768]{2,1,0:T(8,128)(2,1)S(1)}, bf16[4,64,768]{2,1,0:T(8,128)(2,1)S(1)}, u32[]{:S(2)}, u32[]{:S(2)}) collective-permute-start(bf16[4,64,768]{2,1,0:T(8,128)(2,1)S(1)} %collective-permute-done.17.refs_0_), channel_id=1, source_target_pairs={{0,64},{64,128},{128,192},{192,0},{1,65},{65,129},{129,193},{193,1... | collective-permute-start | bytes 1179656 | tf_op jit(solution)/shard_map/ppermute | solution.py:428
  74.8 12.0 %collective-permute-start.19 = (bf16[4,64,768]{2,1,0:T(8,128)(2,1)S(1)}, bf16[4,64,768]{2,1,0:T(8,128)(2,1)S(1)}, u32[]{:S(2)}, u32[]{:S(2)}) collective-permute-start(bf16[4,64,768]{2,1,0:T(8,128)(2,1)S(1)} %collective-permute-done.17.refs_0_), channel_id=1, source_target_pairs={{0,192},{64,0},{128,64},{192,128},{1,193},{65,1},{129,65},{193,129... | collective-permute-start | bytes 1179656 | tf_op jit(solution)/shard_map/ppermute | solution.py:428
  75.7 6.8 %collective-permute-start.14 = (bf16[3,32,384]{2,1,0:T(8,128)(2,1)S(1)}, bf16[3,32,384]{2,1,0:T(8,128)(2,1)S(1)}, u32[]{:S(2)}, u32[]{:S(2)}) collective-permute-start(bf16[3,32,384]{2,1,0:T(8,128)(2,1)S(1)} %get-tuple-element.64), channel_id=1, source_target_pairs={{0,16},{16,32},{32,48},{48,0},{1,17},{17,33},{33,49},{49,1},{2,18}... | collective-permute-start | bytes 221192 | tf_op jit(solution)/shard_map/ppermute | solution.py:428
  79.5 6.4 %collective-permute-start.15 = (bf16[3,32,384]{2,1,0:T(8,128)(2,1)S(1)}, bf16[3,32,384]{2,1,0:T(8,128)(2,1)S(1)}, u32[]{:S(2)}, u32[]{:S(2)}) collective-permute-start(bf16[3,32,384]{2,1,0:T(8,128)(2,1)S(1)} %get-tuple-element.65), channel_id=1, source_target_pairs={{0,32},{16,48},{32,0},{48,16},{1,33},{17,49},{33,1},{49,17},{2,34}... | collective-permute-start | bytes 221192 | tf_op jit(solution)/shard_map/ppermute | solution.py:428
  80.2 5.7 %collective-permute-start.16 = (bf16[3,32,384]{2,1,0:T(8,128)(2,1)S(1)}, bf16[3,32,384]{2,1,0:T(8,128)(2,1)S(1)}, u32[]{:S(2)}, u32[]{:S(2)}) collective-permute-start(bf16[3,32,384]{2,1,0:T(8,128)(2,1)S(1)} %get-tuple-element.66), channel_id=1, source_target_pairs={{0,48},{16,0},{32,16},{48,32},{1,49},{17,1},{33,17},{49,33},{2,50}... | collective-permute-start | bytes 221192 | tf_op jit(solution)/shard_map/ppermute | solution.py:428
  86.5 10.1 %collective-permute-start.25 = (bf16[4,64,768]{2,1,0:T(8,128)(2,1)S(1)}, bf16[4,64,768]{2,1,0:T(8,128)(2,1)S(1)}, u32[]{:S(2)}, u32[]{:S(2)}) collective-permute-start(bf16[4,64,768]{2,1,0:T(8,128)(2,1)S(1)} %collective-permute-done.17.refs_0_), channel_id=1, source_target_pairs={{0,128},{64,192},{128,0},{192,64},{1,129},{65,193},{129,1},{193,65... | collective-permute-start | bytes 1179656 | tf_op jit(solution)/shard_map/ppermute | solution.py:428
  86.9 6.5 %collective-permute-start.20 = (bf16[3,32,384]{2,1,0:T(8,128)(2,1)S(1)}, bf16[3,32,384]{2,1,0:T(8,128)(2,1)S(1)}, u32[]{:S(2)}, u32[]{:S(2)}) collective-permute-start(bf16[3,32,384]{2,1,0:T(8,128)(2,1)S(1)} %add_and_cut.5), channel_id=1, source_target_pairs={{0,16},{16,32},{32,48},{48,0},{1,17},{17,33},{33,49},{49,1},{2,18}... | collective-permute-start | bytes 221192 | tf_op jit(solution)/shard_map/ppermute | solution.py:428
  88.3 7.1 %collective-permute-start.21 = (bf16[3,32,384]{2,1,0:T(8,128)(2,1)S(1)}, bf16[3,32,384]{2,1,0:T(8,128)(2,1)S(1)}, u32[]{:S(2)}, u32[]{:S(2)}) collective-permute-start(bf16[3,32,384]{2,1,0:T(8,128)(2,1)S(1)} %add_and_cut.5), channel_id=1, source_target_pairs={{0,32},{16,48},{32,0},{48,16},{1,33},{17,49},{33,1},{49,17},{2,34}... | collective-permute-start | bytes 221192 | tf_op jit(solution)/shard_map/ppermute | solution.py:428
  89.6 5.8 %collective-permute-start.22 = (bf16[3,32,384]{2,1,0:T(8,128)(2,1)S(1)}, bf16[3,32,384]{2,1,0:T(8,128)(2,1)S(1)}, u32[]{:S(2)}, u32[]{:S(2)}) collective-permute-start(bf16[3,32,384]{2,1,0:T(8,128)(2,1)S(1)} %add_and_cut.5), channel_id=1, source_target_pairs={{0,48},{16,0},{32,16},{48,32},{1,49},{17,1},{33,17},{49,33},{2,50}... | collective-permute-start | bytes 221192 | tf_op jit(solution)/shard_map/ppermute | solution.py:428
  90.9 7.1 %collective-permute-start.23 = (bf16[4,64,768]{2,1,0:T(8,128)(2,1)S(1)}, bf16[4,64,768]{2,1,0:T(8,128)(2,1)S(1)}, u32[]{:S(2)}, u32[]{:S(2)}) collective-permute-start(bf16[4,64,768]{2,1,0:T(8,128)(2,1)S(1)} %collective-permute-done.17.refs_0_), channel_id=1, source_target_pairs={{0,8},{8,0},{1,9},{9,1},{2,10},{10,2},{3,11},{11,3},{4,12},{12,4},... | collective-permute-start | bytes 1179656 | tf_op jit(solution)/shard_map/ppermute | solution.py:432
  93.4 5.6 %collective-permute-start.24 = (bf16[4,64,768]{2,1,0:T(8,128)(2,1)S(1)}, bf16[4,64,768]{2,1,0:T(8,128)(2,1)S(1)}, u32[]{:S(2)}, u32[]{:S(2)}) collective-permute-start(bf16[4,64,768]{2,1,0:T(8,128)(2,1)S(1)} %collective-permute-done.18.refs_2_), channel_id=1, source_target_pairs={{0,8},{8,0},{1,9},{9,1},{2,10},{10,2},{3,11},{11,3},{4,12},{12,4},... | collective-permute-start | bytes 1179656 | tf_op jit(solution)/shard_map/ppermute | solution.py:432
  95.3 5.0 %collective-permute-start.27 = (bf16[4,64,768]{2,1,0:T(8,128)(2,1)S(1)}, bf16[4,64,768]{2,1,0:T(8,128)(2,1)S(1)}, u32[]{:S(2)}, u32[]{:S(2)}) collective-permute-start(bf16[4,64,768]{2,1,0:T(8,128)(2,1)S(1)} %collective-permute-done.19.refs_6_), channel_id=1, source_target_pairs={{0,8},{8,0},{1,9},{9,1},{2,10},{10,2},{3,11},{11,3},{4,12},{12,4},... | collective-permute-start | bytes 1179656 | tf_op jit(solution)/shard_map/ppermute | solution.py:432
  96.6 9.8 %collective-permute-start.33 = (bf16[4,3,32,384]{3,2,1,0:T(8,128)(2,1)S(1)}, bf16[4,3,32,384]{3,2,1,0:T(8,128)(2,1)S(1)}, u32[]{:S(2)}, u32[]{:S(2)}) collective-permute-start(bf16[4,3,32,384]{3,2,1,0:T(8,128)(2,1)S(1)} %pad_maximum_fusion.refs_0_), channel_id=1, source_target_pairs={{0,192},{64,0},{128,64},{192,128},{1,193},{65,1},{129,65},{193,129... | collective-permute-start | bytes 884744 | tf_op jit(solution)/shard_map/ppermute | solution.py:428
  98.0 11.5 %collective-permute-start.31 = (bf16[4,3,32,384]{3,2,1,0:T(8,128)(2,1)S(1)}, bf16[4,3,32,384]{3,2,1,0:T(8,128)(2,1)S(1)}, u32[]{:S(2)}, u32[]{:S(2)}) collective-permute-start(bf16[4,3,32,384]{3,2,1,0:T(8,128)(2,1)S(1)} %pad_maximum_fusion.refs_0_), channel_id=1, source_target_pairs={{0,128},{64,192},{128,0},{192,64},{1,129},{65,193},{129,1},{193,65... | collective-permute-start | bytes 884744 | tf_op jit(solution)/shard_map/ppermute | solution.py:428
  98.9 15.7 %collective-permute-start.29 = (bf16[4,3,32,384]{3,2,1,0:T(8,128)(2,1)S(1)}, bf16[4,3,32,384]{3,2,1,0:T(8,128)(2,1)S(1)}, u32[]{:S(2)}, u32[]{:S(2)}) collective-permute-start(bf16[4,3,32,384]{3,2,1,0:T(8,128)(2,1)S(1)} %pad_maximum_fusion.refs_0_), channel_id=1, source_target_pairs={{0,64},{64,128},{128,192},{192,0},{1,65},{65,129},{129,193},{193,1... | collective-permute-start | bytes 884744 | tf_op jit(solution)/shard_map/ppermute | solution.py:428
  100.3 14.3 %collective-permute-start.28 = (bf16[4,3,32,384]{3,2,1,0:T(8,128)(2,1)S(1)}, bf16[4,3,32,384]{3,2,1,0:T(8,128)(2,1)S(1)}, u32[]{:S(2)}, u32[]{:S(2)}) collective-permute-start(bf16[4,3,32,384]{3,2,1,0:T(8,128)(2,1)S(1)} %pad_maximum_fusion.refs_0_), channel_id=1, source_target_pairs={{0,8},{8,0},{1,9},{9,1},{2,10},{10,2},{3,11},{11,3},{4,12},{12,4},... | collective-permute-start | bytes 884744 | tf_op jit(solution)/shard_map/ppermute | solution.py:432
  106.4 8.2 %collective-permute-start.34 = (bf16[4,3,32,384]{3,2,1,0:T(8,128)(2,1)S(1)}, bf16[4,3,32,384]{3,2,1,0:T(8,128)(2,1)S(1)}, u32[]{:S(2)}, u32[]{:S(2)}) collective-permute-start(bf16[4,3,32,384]{3,2,1,0:T(8,128)(2,1)S(1)} %collective-permute-done.33.refs_6_), channel_id=1, source_target_pairs={{0,8},{8,0},{1,9},{9,1},{2,10},{10,2},{3,11},{11,3},{4,12},{12,4},... | collective-permute-start | bytes 884744 | tf_op jit(solution)/shard_map/ppermute | solution.py:432
  109.5 5.1 %collective-permute-start.32 = (bf16[4,3,32,384]{3,2,1,0:T(8,128)(2,1)S(1)}, bf16[4,3,32,384]{3,2,1,0:T(8,128)(2,1)S(1)}, u32[]{:S(2)}, u32[]{:S(2)}) collective-permute-start(bf16[4,3,32,384]{3,2,1,0:T(8,128)(2,1)S(1)} %collective-permute-done.31.refs_4_), channel_id=1, source_target_pairs={{0,8},{8,0},{1,9},{9,1},{2,10},{10,2},{3,11},{11,3},{4,12},{12,4},... | collective-permute-start | bytes 884744 | tf_op jit(solution)/shard_map/ppermute | solution.py:432
  (16 other events, 26.8 us)
